TPU v7x, 512 devices: a whole 4x8x8 slice. The times are simulated.
512 devices in a mesh: dp: 8 (over y_lo, core), row: 8 (over y_hi, x), col: 8 (over z).
Axes of the slice: x: 4, y: 8 (y_hi: 2, y_lo: 4; y = y_hi * 4 + y_lo), z: 8, core: 2. Of those that a mesh axis runs over, the one named last changes fastest.
Arguments:
- tokens: bfloat16 [1024, 9216], P('dp', 'row'), may hold values from -6 to 6
- weight_in: bfloat16 [9216, 24576], P('row', ('dp', 'col')), may hold values from -0.0625 to 0.0625
- weight_out: bfloat16 [24576, 9216], P(('dp', 'col'), 'row'), may hold values from -0.0390625 to 0.0390625
- grad_out: bfloat16 [1024, 9216], P('dp', 'row'), may hold values from -1.5 to 1.5
Outputs:
- layer_out: bfloat16 [1024, 9216], P(('dp', 'col'), 'row')
- grad_tokens: bfloat16 [1024, 9216], P(('dp', 'col'), 'row')
- grad_weight_in: bfloat16 [9216, 24576], P('row', ('dp', 'col'))
- grad_weight_out: bfloat16 [24576, 9216], P(('dp', 'col'), 'row')
All inputs are finite; a program needn't handle non-finite values.
Results may differ from a plain program's by a relative error of at most 0.025.
Values may be sent and summed in bfloat16 or wider, within the bound.
A program may use at most 64 MiB of HBM per device.

v0:
```python
import jax
import jax.numpy as jnp
from jax import lax
from jax.sharding import PartitionSpec as P


def gelu_value(pre_value):
    inner_arg = 0.7978845608 * (pre_value + 0.044715 * pre_value * pre_value * pre_value)
    return 0.5 * pre_value * (1.0 + jnp.tanh(inner_arg))


def gelu_slope(pre_value):
    tanh_part = jnp.tanh(0.7978845608 * (pre_value + 0.044715 * pre_value * pre_value * pre_value))
    inner_slope = 0.7978845608 * (1.0 + 0.134145 * pre_value * pre_value)
    return 0.5 * (1.0 + tanh_part) + 0.5 * pre_value * (1.0 - tanh_part * tanh_part) * inner_slope


def right_product(source, matrix):
    return jnp.dot(source, matrix, preferred_element_type=jnp.float32)


def right_transposed(source, matrix):
    return lax.dot_general(
        source, matrix, (((1,), (1,)), ((), ())), preferred_element_type=jnp.float32
    )


def shards(tokens, weight_in, weight_out, grad_out):
    all_tokens, all_grads = (
        lax.all_gather(tokens, "dp", axis=0, tiled=True),
        lax.all_gather(grad_out, "dp", axis=0, tiled=True),
    )
    in_tile, out_tile = (
        lax.all_gather(weight_in, "dp", axis=1, tiled=True),
        lax.all_gather(weight_out, "dp", axis=0, tiled=True),
    )
    pre_act = lax.psum_scatter(
        right_product(tokens, in_tile).astype(jnp.bfloat16), "row", scatter_dimension=0, tiled=True
    ).astype(jnp.float32)
    grad_pre = lax.psum_scatter(
        right_transposed(grad_out, out_tile).astype(jnp.bfloat16),
        "row",
        scatter_dimension=0,
        tiled=True,
    ).astype(jnp.float32)
    hidden = gelu_value(pre_act).astype(jnp.bfloat16)
    hidden_block = lax.all_gather(hidden, "row", axis=0, tiled=True)
    grad_act = (grad_pre * gelu_slope(pre_act)).astype(jnp.bfloat16)
    grad_act_block = lax.all_gather(grad_act, "row", axis=0, tiled=True)
    layer_out = lax.psum_scatter(
        right_product(hidden_block, out_tile).astype(jnp.bfloat16),
        "col",
        scatter_dimension=0,
        tiled=True,
    )
    grad_tokens = lax.psum_scatter(
        right_transposed(grad_act_block, in_tile).astype(jnp.bfloat16),
        "col",
        scatter_dimension=0,
        tiled=True,
    )
    hidden_units, grad_units = (
        lax.all_to_all(hidden_block, "dp", split_axis=1, concat_axis=0, tiled=True),
        lax.all_to_all(grad_act_block, "dp", split_axis=1, concat_axis=0, tiled=True),
    )
    grad_weight_in = lax.dot_general(
        all_tokens, grad_units, (((0,), (0,)), ((), ())), preferred_element_type=jnp.float32
    ).astype(jnp.bfloat16)
    grad_weight_out = lax.dot_general(
        hidden_units, all_grads, (((0,), (0,)), ((), ())), preferred_element_type=jnp.float32
    ).astype(jnp.bfloat16)
    return (layer_out, grad_tokens, grad_weight_in, grad_weight_out)


def solution(mesh):
    placed = (P("dp", "row"), P("row", ("dp", "col")), P(("dp", "col"), "row"), P("dp", "row"))
    return jax.shard_map(
        shards,
        mesh=mesh,
        in_specs=placed,
        out_specs=(
            P(("dp", "col"), "row"),
            P(("dp", "col"), "row"),
            P("row", ("dp", "col")),
            P(("dp", "col"), "row"),
        ),
        check_vma=False,
    )
```

profile of v0, /device:TPU:4, one launch (start us, length us, event | category | flops | bytes accessed | tf_op | source)
XLA Modules:
  0.0 588.7 jit_solution(16831372559027952307)
XLA Ops:
  7.2 0.0 all-gather.5.cloned.1.call-start
  7.2 0.7 all-gather.5.cloned.1.call-update
  7.9 0.0 all-gather.7.cloned.1.call-start
  7.9 0.7 all-gather.7.cloned.1.call-update
  8.7 0.0 reduce-scatter.5.cloned.1.call-start
  8.7 90.4 %all-gather.5.cloned.1.call-done = bf16[1152,3072]{1,0:T(8,128)(2,1)} async-done(((bf16[1152,384]{1,0:T(8,128)(2,1)}), bf16[1152,3072]{1,0:T(8,128)(2,1)}) %all-gather.5.cloned.1.call-update) | async-done | bytes 7077904 | tf_op jit(solution)/shard_map/all_gather | solution.py:34
  99.1 5.2 convolution_convert_fusion.1
  104.3 0.0 reduce-scatter.9.cloned.1.call-start
  104.3 79.8 %all-gather.7.cloned.1.call-done = bf16[3072,1152]{1,0:T(8,128)(2,1)} async-done(((bf16[384,1152]{1,0:T(8,128)(2,1)}), bf16[3072,1152]{1,0:T(8,128)(2,1)}) %all-gather.7.cloned.1.call-update) | async-done | bytes 7077904 | tf_op jit(solution)/shard_map/all_gather | solution.py:35
  184.1 6.3 %convolution_convert_fusion = bf16[128,3072]{1,0:T(8,128)(2,1)} fusion(bf16[128,1152]{1,0:T(8,128)(2,1)S(1)} %copy-done, bf16[3072,1152]{1,0:T(8,128)(2,1)} %all-gather.7.cloned.1.call-done), kind=kOutput, calls=%fused_computation | convolution fusion | flops 906362880 | bytes 8159232 | tf_op jit(solution)/shard_map/dot_general | solution.py:23
  190.4 0.0 all-gather.9.cloned.1.call-start
  190.5 0.5 all-gather.9.cloned.1.call-update
  191.0 0.0 all-gather.11.cloned.1.call-start
  191.1 0.5 all-gather.11.cloned.1.call-update
  191.6 85.4 %reduce-scatter.5.cloned.1.call-done = bf16[16,3072]{1,0:T(8,128)(2,1)} async-done(((bf16[128,3072]{1,0:T(8,128)(2,1)}), bf16[16,3072]{1,0:T(8,128)(2,1)}) %reduce-scatter.5.cloned.1.call-update) | async-done | bytes 98320 | tf_op jit(solution)/shard_map/reduce_scatter | solution.py:37
  277.0 91.6 %reduce-scatter.9.cloned.1.call-done = bf16[16,3072]{1,0:T(8,128)(2,1)} async-done(((bf16[128,3072]{1,0:T(8,128)(2,1)}), bf16[16,3072]{1,0:T(8,128)(2,1)}) %reduce-scatter.9.cloned.1.call-update) | async-done | bytes 98320 | tf_op jit(solution)/shard_map/reduce_scatter | solution.py:40
  368.6 1.1 fusion.7
  369.7 44.1 %all_gather.21 = bf16[128,3072]{1,0:T(8,128)(2,1)S(1)} all-gather(bf16[16,3072]{1,0:T(8,128)(2,1)S(1)} %get-tuple-element.12), channel_id=1, replica_groups=mesh['dp'=8,'row'=8,'col'=8] {'row'}, dimensions={0}, use_global_device_ids=true | all-gather | bytes 884736 | tf_op jit(solution)/shard_map/all_gather | solution.py:49
  413.8 1.0 copy.17
  414.7 4.5 all-to-all-start
  419.3 64.6 %all_gather.19 = bf16[128,3072]{1,0:T(8,128)(2,1)S(1)} all-gather(bf16[16,3072]{1,0:T(8,128)(2,1)S(1)} %get-tuple-element.13), channel_id=1, replica_groups=mesh['dp'=8,'row'=8,'col'=8] {'row'}, dimensions={0}, use_global_device_ids=true | all-gather | bytes 884736 | tf_op jit(solution)/shard_map/all_gather | solution.py:47
  483.9 1.0 copy.16
  484.8 7.8 %all-to-all-start.1 = ((bf16[128,8,384]{2,0,1:T(8,128)(2,1)}), bf16[128,8,384]{2,0,1:T(8,128)(2,1)S(1)}, u32[]{:S(2)}, u32[]{:S(2)}) async-start(bf16[128,8,384]{2,0,1:T(8,128)(2,1)} %bitcast.26), calls=%async_computation.5 | async-start | bytes 1572864 | tf_op jit(solution)/shard_map/all_to_all | solution.py:63
  492.6 6.1 %convolution_convert_fusion.4 = bf16[128,1152]{1,0:T(8,128)(2,1)} fusion(bf16[128,3072]{1,0:T(8,128)(2,1)S(1)} %all_gather.21, bf16[1152,3072]{1,0:T(8,128)(2,1)} %all-gather.5.cloned.1.call-done), kind=kOutput, calls=%fused_computation.5 | convolution fusion | flops 906117120 | bytes 8159232 | tf_op jit(solution)/shard_map/dot_general | solution.py:23
  498.7 0.0 reduce-scatter.7.cloned.1.call-start
  498.8 4.9 convolution_convert_fusion.5
  503.8 2.9 fusion
  506.7 1.3 copy.11
  508.0 5.6 all-to-all-done.1
  513.6 3.8 convolution_convert_fusion.2
  517.4 22.4 %reduce-scatter.11.cloned.1.call-done = bf16[16,1152]{1,0:T(8,128)(2,1)} async-done(((bf16[128,1152]{1,0:T(8,128)(2,1)}), bf16[16,1152]{1,0:T(8,128)(2,1)}) %reduce-scatter.11.cloned.1.call-update) | async-done | bytes 36880 | tf_op jit(solution)/shard_map/reduce_scatter | solution.py:56
  539.8 42.1 %reduce-scatter.7.cloned.1.call-done = bf16[16,1152]{1,0:T(8,128)(2,1)} async-done(((bf16[128,1152]{1,0:T(8,128)(2,1)}), bf16[16,1152]{1,0:T(8,128)(2,1)}) %reduce-scatter.7.cloned.1.call-update) | async-done | bytes 36880 | tf_op jit(solution)/shard_map/reduce_scatter | solution.py:50
  (10 shorter events, 0.1 us)
Async XLA Ops:
  7.2 91.9 %all-gather.5.cloned.1.call-start = ((), (), s32[]{:S(2)}) async-start(), calls=%async_computation.6 | async-start | bytes 7962624 | tf_op jit(solution)/shard_map/all_gather | solution.py:34
  7.9 176.2 %all-gather.7.cloned.1.call-start = ((), (), s32[]{:S(2)}) async-start(), calls=%async_computation.8 | async-start | bytes 7962624 | tf_op jit(solution)/shard_map/all_gather | solution.py:35
  8.6 175.5 %copy-start = (bf16[128,1152]{1,0:T(8,128)(2,1)S(1)}, bf16[128,1152]{1,0:T(8,128)(2,1)}, u32[]{:S(2)}) copy-start(bf16[128,1152]{1,0:T(8,128)(2,1)} %param.7) | copy-start | bytes 884740
  8.7 268.3 %reduce-scatter.5.cloned.1.call-start = ((), (), s32[]{:S(2)}) async-start(), calls=%async_computation.7 | async-start | bytes 884736 | tf_op jit(solution)/shard_map/reduce_scatter | solution.py:37
  104.3 264.3 %reduce-scatter.9.cloned.1.call-start = ((), (), s32[]{:S(2)}) async-start(), calls=%async_computation.10 | async-start | bytes 884736 | tf_op jit(solution)/shard_map/reduce_scatter | solution.py:40
  190.4 313.3 %all-gather.9.cloned.1.call-start = ((), (), s32[]{:S(2)}) async-start(), calls=%async_computation.12 | async-start | bytes 2654208 | tf_op jit(solution)/shard_map/all_gather | solution.py:30
  191.0 317.0 %all-gather.11.cloned.1.call-start = ((), (), s32[]{:S(2)}) async-start(), calls=%async_computation.13 | async-start | bytes 2654208 | tf_op jit(solution)/shard_map/all_gather | solution.py:31
  414.7 70.1 %all-to-all-start = ((bf16[128,8,384]{2,0,1:T(8,128)(2,1)}), bf16[128,8,384]{2,0,1:T(8,128)(2,1)S(1)}, u32[]{:S(2)}, u32[]{:S(2)}) async-start(bf16[128,8,384]{2,0,1:T(8,128)(2,1)} %bitcast.27), calls=%async_computation.4 | async-start | bytes 1572864 | tf_op jit(solution)/shard_map/all_to_all | solution.py:64
  484.8 28.7 %all-to-all-start.1 = ((bf16[128,8,384]{2,0,1:T(8,128)(2,1)}), bf16[128,8,384]{2,0,1:T(8,128)(2,1)S(1)}, u32[]{:S(2)}, u32[]{:S(2)}) async-start(bf16[128,8,384]{2,0,1:T(8,128)(2,1)} %bitcast.26), calls=%async_computation.5 | async-start | bytes 1572864 | tf_op jit(solution)/shard_map/all_to_all | solution.py:63
  492.6 47.2 %reduce-scatter.11.cloned.1.call-start = ((), (), s32[]{:S(2)}) async-start(), calls=%async_computation.11 | async-start | bytes 331776 | tf_op jit(solution)/shard_map/reduce_scatter | solution.py:56
  498.7 83.1 %reduce-scatter.7.cloned.1.call-start = ((), (), s32[]{:S(2)}) async-start(), calls=%async_computation.9 | async-start | bytes 331776 | tf_op jit(solution)/shard_map/reduce_scatter | solution.py:50
Sparse Core Ops, SparseCore 0:
  10.1 88.9 all-gather.4
  101.2 82.9 all-gather.6
  189.2 87.7 reduce-scatter.4
  281.9 86.5 reduce-scatter.8
  370.5 39.7 all-gather.8
  412.2 50.1 all-gather.10
  498.9 40.9 reduce-scatter.10
  543.4 38.4 reduce-scatter.6
where the time goes:
time: 589 us
  waiting for transfers between devices  420 us (71%)
  blocking collectives  109 us (19%)
  matrix products  29.1 us (5%)
  between operations  14.2 us (2%)
  starting transfers between devices  12.6 us (2%)
    reduce_scatter x1, waiting for transfers between devices, shards(): lax.psum_scatter(right_transposed(grad_out, out_tile).astype(jnp.bfloat16...  91.6 us
    all_gather x1, waiting for transfers between devices, shards(): lax.all_gather(weight_in, 'dp', axis=1, tiled=True)  90.4 us
    reduce_scatter x1, waiting for transfers between devices, shards(): lax.psum_scatter(right_product(tokens, in_tile).astype(jnp.bfloat16), 'ro...  85.4 us
    all_gather x1, waiting for transfers between devices, shards(): lax.all_gather(weight_out, 'dp', axis=0, tiled=True)  79.8 us
    all_gather x1, blocking collectives, shards(): hidden_block = lax.all_gather(hidden, 'row', axis=0, tiled=True)  64.6 us
    all_gather x1, blocking collectives, shards(): grad_act_block = lax.all_gather(grad_act, 'row', axis=0, tiled=True)  44.1 us
    reduce_scatter x1, waiting for transfers between devices, shards(): lax.psum_scatter(right_product(hidden_block, out_tile).astype(jnp.bfloat1...  42.1 us
    reduce_scatter x1, waiting for transfers between devices, shards(): lax.psum_scatter(right_transposed(grad_act_block, in_tile).astype(jnp.bfl...  22.4 us
  transfers between devices with their start and end apart: 10, of which 7 were waited for; matrix products, arithmetic and copies ran while one was open for 6% of the time, Pallas kernels for 0%

commit v1 on v0

v1 whole, which is shorter than its diff:
```python
import functools

import jax
import jax.numpy as jnp
from jax import lax
from jax.experimental import pallas as pl
from jax.experimental.pallas import tpu as pltpu
from jax.sharding import PartitionSpec as P

MESH = pl.DeviceIdType.MESH
BF16 = jnp.bfloat16
F32 = jnp.float32

PLACE = {0: 0, 1: 1, 7: 2, 2: 3, 6: 4, 3: 5, 5: 6, 4: 7}
GROUPS = ((0, 1), (1, 2), (3, 2), (5, 2), (7, 1))


def gelu_value(pre_value):
    inner_arg = 0.7978845608 * (pre_value + 0.044715 * pre_value * pre_value * pre_value)
    return 0.5 * pre_value * (1.0 + jnp.tanh(inner_arg))


def gelu_slope(pre_value):
    tanh_part = jnp.tanh(0.7978845608 * (pre_value + 0.044715 * pre_value * pre_value * pre_value))
    inner_slope = 0.7978845608 * (1.0 + 0.134145 * pre_value * pre_value)
    return 0.5 * (1.0 + tanh_part) + 0.5 * pre_value * (1.0 - tanh_part * tanh_part) * inner_slope


def kernel(
    tokens, weight_in, weight_out, grad_out,
    layer_out, grad_tokens, grad_weight_in, grad_weight_out,
    TK, X, WI, WO, PS, PR, YS, YR, HC, SS, SR, OP, ZS, ZRR, ZRL, FS, FR, FO, OB, GI, GO,
    local_sem, a_send, a_recv, j_send, j_recv, c_send, c_recv, r_send, r_recv, l_send, l_recv,
    p_send, p_recv, y_send, y_recv, h_send, h_recv, s_send, s_recv,
    zr_send, zr_recv, zl_send, zl_recv, f_send, f_recv,
):
    dp = lax.axis_index("dp")
    row = lax.axis_index("row")
    z = lax.axis_index("col")
    y, core = dp // 2, dp % 2
    half, x = row // 4, row % 4

    def device(dp=dp, row=row, col=z):
        return {"dp": dp, "row": row, "col": col}

    sibling = device(dp=y * 2 + (1 - core))
    right, left = device(col=(z + 1) % 8), device(col=(z + 7) % 8)
    across = device(row=(1 - half) * 4 + x)
    y_peers = {j: device(dp=((y + j) % 4) * 2 + core) for j in (1, 2, 3)}
    x_of = {m: (x + m) % 4 for m in (1, 2, 3)}
    x_peers = {m: device(row=half * 4 + x_of[m]) for m in (1, 2, 3)}

    pending = []

    def send(src, dst, ssem, rsem, to):
        copy = pltpu.make_async_remote_copy(
            src_ref=src, dst_ref=dst, send_sem=ssem, recv_sem=rsem, device_id=to, device_id_type=MESH
        )
        copy.start()
        pending.append(copy)

    def arrived(dst, ssem, rsem):
        pltpu.make_async_remote_copy(
            src_ref=dst, dst_ref=dst, send_sem=ssem, recv_sem=rsem, device_id=sibling, device_id_type=MESH
        ).wait_recv()

    fetch = [
        pltpu.make_async_copy(tokens, TK.at[0], local_sem.at[0]),
        pltpu.make_async_copy(grad_out, TK.at[1], local_sem.at[1]),
        pltpu.make_async_copy(weight_in, WI, local_sem.at[2]),
        pltpu.make_async_copy(weight_out, WO, local_sem.at[3]),
    ]
    for copy in fetch:
        copy.start()

    barrier = pltpu.get_barrier_semaphore()
    peers = [sibling, right, left, across, *y_peers.values(), *x_peers.values()]
    for peer in peers:
        pl.semaphore_signal(barrier, inc=1, device_id=peer, device_id_type=MESH)
    pl.semaphore_wait(barrier, len(peers))

    fetch[0].wait()
    fetch[1].wait()
    for j in (1, 2, 3):
        send(TK.at[:, z], X.at[0, :, pl.ds((4 - j) * 16, 16)], a_send.at[j - 1], a_recv.at[3 - j], y_peers[j])
    for r in range(8):
        for a in range(2):
            X[PLACE[r], a, 0:16] = TK[a, (z + r) % 8]
    send(X.at[:, :, 0:16], X.at[:, :, 64:80], j_send, j_recv, sibling)
    fetch[2].wait()
    fetch[3].wait()

    def to_sibling(g):
        q, n = GROUPS[g]
        send(X.at[pl.ds(q, n), :, 16:64], X.at[pl.ds(q, n), :, 80:128], c_send.at[g], c_recv.at[g], sibling)

    def stage_c(g):
        q, n = GROUPS[g]
        if g == 0:
            arrived(X.at[:, :, 64:80], j_send, j_recv)
        arrived(X.at[pl.ds(q, n), :, 80:128], c_send.at[g], c_recv.at[g])
        lhs = X[q:q + n, 0].reshape(n * 128, 1152)
        val = jnp.dot(lhs, WI[...], preferred_element_type=F32).astype(BF16).reshape(n, 4, 32, 384)
        for p in range(4):
            PS[p, q:q + n, 0] = val[:, p]
        lhs = X[q:q + n, 1].reshape(n * 128, 1152)
        val = lax.dot_general(lhs, WO[...], (((1,), (1,)), ((), ())), preferred_element_type=F32)
        val = val.astype(BF16).reshape(n, 4, 32, 384)
        for p in range(4):
            PS[p, q:q + n, 1] = val[:, p]
        for m in (1, 2, 3):
            send(
                PS.at[x_of[m], pl.ds(q, n)], PR.at[m - 1, pl.ds(q, n)],
                p_send.at[g * 3 + m - 1], p_recv.at[g * 3 + m - 1], x_peers[m],
            )

    def stage_d(g):
        q, n = GROUPS[g]
        total = PS[x, q:q + n].astype(F32)
        for m in (1, 2, 3):
            arrived(PR.at[m - 1, pl.ds(q, n)], p_send.at[g * 3 + m - 1], p_recv.at[g * 3 + m - 1])
            total = total + PR[m - 1, q:q + n].astype(F32)
        YS[q:q + n] = total.astype(BF16)
        send(YS.at[pl.ds(q, n)], YR.at[pl.ds(q, n)], y_send.at[g], y_recv.at[g], across)

    def stage_e(g):
        q, n = GROUPS[g]
        arrived(YR.at[pl.ds(q, n)], y_send.at[g], y_recv.at[g])
        pre = YS[q:q + n, 0].astype(F32) + YR[q:q + n, 0].astype(F32)
        grad = YS[q:q + n, 1].astype(F32) + YR[q:q + n, 1].astype(F32)
        HC[q:q + n, 0, x] = gelu_value(pre).astype(BF16)
        HC[q:q + n, 1, x] = (grad * gelu_slope(pre)).astype(BF16)
        for m in (1, 2, 3):
            send(
                HC.at[pl.ds(q, n), :, x], HC.at[pl.ds(q, n), :, x],
                h_send.at[g * 3 + m - 1], h_recv.at[g * 3 + m - 1], x_peers[m],
            )

    def stage_f(g):
        q, n = GROUPS[g]
        for m in (1, 2, 3):
            arrived(HC.at[pl.ds(q, n), :, (x + 4 - m) % 4], h_send.at[g * 3 + m - 1], h_recv.at[g * 3 + m - 1])
        for a in range(2):
            lhs = HC[q:q + n, a].reshape(n * 128, 384)
            if a == 0:
                val = jnp.dot(lhs, WO[...], preferred_element_type=F32)
            else:
                val = lax.dot_general(lhs, WI[...], (((1,), (1,)), ((), ())), preferred_element_type=F32)
            val = val.reshape(n, 2, 64, 1152)
            OP[q:q + n, a] = val[:, 0]
            SS[q:q + n, a] = val[:, 1].astype(BF16)
        send(SS.at[pl.ds(q, n)], SR.at[pl.ds(q, n)], s_send.at[g], s_recv.at[g], sibling)

    def both_cores(r, a):
        return OP[PLACE[r], a] + SR[PLACE[r], a].astype(F32)

    def go_right(r, a):
        send(ZS.at[PLACE[r], a], ZRR.at[r - 1, a], zr_send.at[r * 2 + a], zr_recv.at[r * 2 + a], right)

    def go_left(r, a):
        send(ZS.at[PLACE[r], a], ZRL.at[r - 4, a], zl_send.at[(r - 4) * 2 + a], zl_recv.at[(r - 4) * 2 + a], left)

    def from_left(r, a):
        arrived(ZRR.at[r, a], zr_send.at[(r + 1) * 2 + a], zr_recv.at[(r + 1) * 2 + a])
        return ZRR[r, a].astype(F32)

    def from_right(r, a):
        arrived(ZRL.at[r - 5, a], zl_send.at[(r - 5) * 2 + a], zl_recv.at[(r - 5) * 2 + a])
        return ZRL[r - 5, a].astype(F32)

    def stage_g(g):
        q, n = GROUPS[g]
        arrived(SR.at[pl.ds(q, n)], s_send.at[g], s_recv.at[g])
        if g == 4:
            ZS[PLACE[4], 0] = both_cores(4, 0).astype(BF16)
            go_right(4, 0)
            ZS[PLACE[4], 1] = both_cores(4, 1).astype(BF16)
            go_left(4, 1)
            return
        for a in (0, 1):
            total = both_cores(g, a)
            if g < 3 or a == 0:
                total = total + from_left(g, a)
            ZS[PLACE[g], a] = total.astype(BF16)
            go_right(g, a)
            b = 1 - a
            total = both_cores(8 - g, b)
            if g < 3 or b == 1:
                total = total + from_right(8 - g, b)
            ZS[PLACE[8 - g], b] = total.astype(BF16)
            go_left(8 - g, b)

    def ring(s, a, going_right):
        if going_right:
            send(
                X.at[PLACE[(8 - s) % 8], a, 16:64], X.at[PLACE[7 - s], a, 16:64],
                r_send.at[s * 2 + a], r_recv.at[s * 2 + a], right,
            )
        else:
            send(
                X.at[PLACE[s], a, 16:64], X.at[PLACE[s + 1], a, 16:64],
                l_send.at[s * 2 + a], l_recv.at[s * 2 + a], left,
            )

    def ring_arrived(s, a, going_right):
        if going_right:
            arrived(X.at[PLACE[7 - s], a, 16:64], r_send.at[s * 2 + a], r_recv.at[s * 2 + a])
        else:
            arrived(X.at[PLACE[s + 1], a, 16:64], l_send.at[s * 2 + a], l_recv.at[s * 2 + a])

    for j in (1, 2, 3):
        arrived(X.at[0, :, pl.ds(j * 16, 16)], a_send.at[j - 1], a_recv.at[j - 1])
    for a in (0, 1):
        ring(0, a, True)
        ring(0, 1 - a, False)
    to_sibling(0)
    stage_c(0)
    for s in (1, 2, 3):
        for a in (0, 1):
            ring_arrived(s - 1, a, True)
            if s < 3 or a == 0:
                ring(s, a, True)
            ring_arrived(s - 1, 1 - a, False)
            if s < 3 or a == 0:
                ring(s, 1 - a, False)
        to_sibling(s)
        stage_d(s - 1)
        stage_c(s)
    ring_arrived(3, 0, True)
    ring_arrived(3, 1, False)
    to_sibling(4)
    stage_d(3)
    stage_c(4)
    stage_d(4)
    for g in (3, 4, 2, 1, 0):
        stage_e(g)
    stage_f(4)
    stage_f(3)
    stage_g(4)
    stage_f(2)
    stage_g(3)
    stage_f(1)
    stage_g(2)
    stage_f(0)
    stage_g(1)

    hidden_all, grad_all = HC[:, 0].reshape(1024, 384), HC[:, 1].reshape(1024, 384)

    @pl.loop(0, 9)
    def _(i):
        cols = pl.ds(pl.multiple_of(i * 128, 128), 128)
        lhs = X[:, 0, :, cols].reshape(1024, 128)
        GI[cols, :] = lax.dot_general(
            lhs, grad_all, (((0,), (0,)), ((), ())), preferred_element_type=F32
        ).astype(BF16)
        rhs = X[:, 1, :, cols].reshape(1024, 128)
        GO[:, cols] = lax.dot_general(
            hidden_all, rhs, (((0,), (0,)), ((), ())), preferred_element_type=F32
        ).astype(BF16)

    stores = [
        pltpu.make_async_copy(GI, grad_weight_in, local_sem.at[4]),
        pltpu.make_async_copy(GO, grad_weight_out, local_sem.at[5]),
    ]
    for copy in stores:
        copy.start()

    arrived(SR.at[pl.ds(0, 1)], s_send.at[0], s_recv.at[0])
    for a in (0, 1):
        total = both_cores(0, a) + from_left(0, a) + from_right(8, a)
        FO[a] = total[0:16]
        for j in (1, 2, 3):
            FS[j - 1, a] = total[j * 16:(j + 1) * 16].astype(BF16)
    for j in (1, 2, 3):
        send(FS.at[j - 1], FR.at[j - 1], f_send.at[j - 1], f_recv.at[j - 1], y_peers[j])
    total = FO[...]
    for j in (1, 2, 3):
        arrived(FR.at[j - 1], f_send.at[j - 1], f_recv.at[j - 1])
        total = total + FR[j - 1].astype(F32)
    OB[...] = total.astype(BF16)
    stores.append(pltpu.make_async_copy(OB.at[0], layer_out, local_sem.at[6]))
    stores.append(pltpu.make_async_copy(OB.at[1], grad_tokens, local_sem.at[7]))
    stores[2].start()
    stores[3].start()
    for copy in pending:
        copy.wait_send()
    for copy in stores:
        copy.wait()


def shards(tokens, weight_in, weight_out, grad_out):
    any_space = pl.BlockSpec(memory_space=pl.ANY)
    dma = pltpu.SemaphoreType.DMA
    return pl.pallas_call(
        kernel,
        out_shape=(
            jax.ShapeDtypeStruct((16, 1152), BF16),
            jax.ShapeDtypeStruct((16, 1152), BF16),
            jax.ShapeDtypeStruct((1152, 384), BF16),
            jax.ShapeDtypeStruct((384, 1152), BF16),
        ),
        in_specs=[any_space] * 4,
        out_specs=(any_space,) * 4,
        scratch_shapes=[
            pltpu.VMEM((2, 8, 16, 1152), BF16),
            pltpu.VMEM((8, 2, 128, 1152), BF16),
            pltpu.VMEM((1152, 384), BF16),
            pltpu.VMEM((384, 1152), BF16),
            pltpu.VMEM((4, 8, 2, 32, 384), BF16),
            pltpu.VMEM((3, 8, 2, 32, 384), BF16),
            pltpu.VMEM((8, 2, 32, 384), BF16),
            pltpu.VMEM((8, 2, 32, 384), BF16),
            pltpu.VMEM((8, 2, 4, 32, 384), BF16),
            pltpu.VMEM((8, 2, 64, 1152), BF16),
            pltpu.VMEM((8, 2, 64, 1152), BF16),
            pltpu.VMEM((8, 2, 64, 1152), F32),
            pltpu.VMEM((8, 2, 64, 1152), BF16),
            pltpu.VMEM((4, 2, 64, 1152), BF16),
            pltpu.VMEM((4, 2, 64, 1152), BF16),
            pltpu.VMEM((3, 2, 16, 1152), BF16),
            pltpu.VMEM((3, 2, 16, 1152), BF16),
            pltpu.VMEM((2, 16, 1152), F32),
            pltpu.VMEM((2, 16, 1152), BF16),
            pltpu.VMEM((1152, 384), BF16),
            pltpu.VMEM((384, 1152), BF16),
            dma((8,)),
            dma((3,)), dma((3,)),
            dma, dma,
            dma((5,)), dma((5,)),
            dma((8,)), dma((8,)),
            dma((8,)), dma((8,)),
            dma((15,)), dma((15,)),
            dma((5,)), dma((5,)),
            dma((15,)), dma((15,)),
            dma((5,)), dma((5,)),
            dma((10,)), dma((10,)),
            dma((8,)), dma((8,)),
            dma((3,)), dma((3,)),
        ],
        compiler_params=pltpu.CompilerParams(
            collective_id=0, has_side_effects=True, vmem_limit_bytes=56 * 1024 * 1024
        ),
        cost_estimate=pl.CostEstimate(flops=5436000000, bytes_accessed=8000000, transcendentals=1000000),
    )(tokens.reshape(8, 16, 1152), weight_in, weight_out, grad_out.reshape(8, 16, 1152))


def solution(mesh):
    placed = (P("dp", "row"), P("row", ("dp", "col")), P(("dp", "col"), "row"), P("dp", "row"))
    return jax.shard_map(
        shards,
        mesh=mesh,
        in_specs=placed,
        out_specs=(
            P(("dp", "col"), "row"),
            P(("dp", "col"), "row"),
            P("row", ("dp", "col")),
            P(("dp", "col"), "row"),
        ),
        check_vma=False,
    )
```

time: 589 us -> 114 us (0.19)
  the two profiles are of different devices: /device:TPU:4 before, /device:TPU:24 now
where the time goes in v1:
time: 114 us
  Pallas kernels  108 us (95%)
  local copies, waits for them, and re-layouts  5.18 us (5%)
    pallas_call x1, Pallas kernels, shards(): pl.pallas_call(kernel, out_shape=(jax.ShapeDtypeStruct((16, 1152), BF16),...  108 us
    unnamed x8, local copies, waits for them, and re-layouts  5.18 us

profile of v1, /device:TPU:24, one launch (start us, length us, event | category | flops | bytes accessed | tf_op | source)
XLA Modules:
  0.0 113.7 jit_solution(16534857059841754423)
XLA Ops:
  0.6 107.9 %shard_map.75 = (bf16[16,1152]{1,0:T(8,128)(2,1)}, bf16[16,1152]{1,0:T(8,128)(2,1)}, bf16[1152,384]{1,0:T(8,128)(2,1)}, bf16[384,1152]{1,0:T(8,128)(2,1)}) custom-call(bf16[8,16,1152]{2,1,0:T(8,128)(2,1)} %bitcast.2, bf16[1152,384]{1,0:T(8,128)(2,1)} %weight_in.1, bf16[384,1152]{1,0:T(8,128)(2,1)} %weight_out.1, bf16[8,16,1152]{2,1,0:T(8,128)(2,1)} %bitcast.3), custom_call_target="tpu_custom_call" | custom-call | flops 5436000256 | bytes 8000000 | tf_op jit(solution)/shard_map/pallas_call | solution.py:294
  108.5 0.0 copy-start.1
  108.5 1.4 %copy.12 = bf16[16,1152]{1,0:T(8,128)(2,1)} copy(bf16[16,1152]{1,0:T(8,128)(2,1)} %get-tuple-element.8) | data formatting | bytes 73728
  109.9 0.0 copy-done.1
  109.9 0.6 copy.13
  110.5 0.0 copy-start
  110.5 2.2 %copy.14 = bf16[1152,384]{1,0:T(8,128)(2,1)} copy(bf16[1152,384]{1,0:T(8,128)(2,1)} %get-tuple-element.10) | data formatting | bytes 1769472
  112.8 0.0 copy-done
  112.8 0.9 copy.15
Async XLA Ops:
  108.5 1.4 %copy-start.1 = (bf16[16,1152]{1,0:T(8,128)(2,1)S(1)}, bf16[16,1152]{1,0:T(8,128)(2,1)}, u32[]{:S(2)}) copy-start(bf16[16,1152]{1,0:T(8,128)(2,1)} %get-tuple-element.9) | copy-start | bytes 110596
  110.5 2.3 %copy-start = (bf16[384,1152]{1,0:T(8,128)(2,1)S(1)}, bf16[384,1152]{1,0:T(8,128)(2,1)}, u32[]{:S(2)}) copy-start(bf16[384,1152]{1,0:T(8,128)(2,1)} %get-tuple-element.11) | copy-start | bytes 2654212

commit v2 on v0

v2 whole, which is shorter than its diff:
```python
import jax
import jax.numpy as jnp
from jax import lax
from jax.experimental import pallas as pl
from jax.experimental.pallas import tpu as pltpu
from jax.sharding import PartitionSpec as P

MESH = pl.DeviceIdType.MESH
BF16 = jnp.bfloat16
F32 = jnp.float32

PLACE = {0: 0, 1: 1, 7: 2, 2: 3, 6: 4, 3: 5, 5: 6, 4: 7}
STEP_PLACES = ((0, 3), (3, 2), (5, 2), (7, 1))

ORDER = (
    ("A",), ("J",), ("Z", 1, 0, "R"), ("Z", 1, 0, "L"), ("C", 0), ("Z", 1, 1, "R"), ("Z", 1, 1, "L"), ("S", 1, 0),
    ("Z", 2, 0, "R"), ("Z", 2, 0, "L"), ("Z", 1, 2, "R"), ("Z", 1, 2, "L"), ("S", 1, 1), ("Z", 3, 0, "R"),
    ("Z", 3, 0, "L"), ("D", 0), ("Z", 2, 1, "R"), ("Z", 2, 1, "L"), ("S", 2, 0), ("Z", 1, 3, "R"),
    ("Z", 1, 3, "L"), ("S", 1, 2), ("Z", 3, 1, "R"), ("Z", 3, 1, "L"), ("S", 3, 0), ("Z", 2, 2, "R"), ("S", 2, 1),
    ("Z", 2, 2, "L"), ("S", 1, 3), ("E", 0), ("Z", 3, 2, "R"), ("C", 1), ("Z", 3, 2, "L"), ("S", 3, 1),
    ("Z", 2, 3, "R"), ("S", 2, 2), ("Z", 2, 3, "L"), ("Z", 3, 3, "R"), ("S", 3, 2), ("Z", 3, 3, "L"), ("S", 2, 3),
    ("F", 0), ("S", 3, 3), ("C", 2), ("R", 0, 0, "R"), ("R", 0, 0, "L"), ("D", 1), ("C", 3), ("R", 0, 1, "R"),
    ("R", 0, 1, "L"), ("D", 2), ("R", 0, 2, "R"), ("R", 0, 2, "L"), ("E", 1), ("R", 0, 3, "R"), ("R", 0, 3, "L"),
    ("D", 3), ("H", 0), ("E", 2), ("F", 1), ("E", 3), ("R", 1, 0, "R"), ("R", 1, 0, "L"), ("F", 2),
    ("R", 1, 1, "R"), ("R", 1, 1, "L"), ("R", 2, 0, "R"), ("R", 2, 0, "L"), ("F", 3), ("R", 2, 1, "R"),
    ("R", 2, 1, "L"), ("W", 0), ("W", 1), ("R", 3, 0, "R"), ("R", 3, 0, "L"), ("W", 2), ("R", 2, 2, "R"),
    ("R", 2, 2, "L"), ("W", 3), ("R", 3, 1, "R"), ("R", 3, 1, "L"), ("W", 4), ("R", 1, 2, "R"), ("R", 1, 2, "L"),
    ("R", 2, 3, "R"), ("R", 2, 3, "L"), ("R", 3, 2, "R"), ("R", 3, 2, "L"), ("R", 1, 3, "R"), ("R", 1, 3, "L"),
    ("H", 2), ("R", 3, 3, "R"), ("R", 3, 3, "L"), ("H", 1), ("H", 3), ("FIN",),
)


def gelu_both(pre_value, grad_value):
    square = pre_value * pre_value
    tanh_part = jnp.tanh(0.7978845608 * (pre_value + 0.044715 * square * pre_value))
    inner_slope = 0.7978845608 * (1.0 + 0.134145 * square)
    value = 0.5 * pre_value * (1.0 + tanh_part)
    slope = 0.5 * (1.0 + tanh_part) + 0.5 * pre_value * (1.0 - tanh_part * tanh_part) * inner_slope
    return value, grad_value * slope


def rows_of(place, count=1):
    return pl.ds(place * 16, count * 16)


def times(left, right):
    return jnp.dot(left, right, preferred_element_type=F32)


def times_transposed(left, right):
    return lax.dot_general(left, right, (((1,), (1,)), ((), ())), preferred_element_type=F32)


def kernel(
    tokens, weight_in, weight_out, grad_out,
    layer_out, grad_tokens, grad_weight_in, grad_weight_out,
    TK, X, WI, WO, PS, PR, YS, YR, HC, HT, GT, SS, SR, OP, ZS, ZR, FS, FR, FO, OB, GI, GO, XA, XB, YT,
    local_sem, a_send, a_recv, j_send, j_recv, c_send, c_recv, z_send, z_recv,
    p_send, p_recv, y_send, y_recv, h_send, h_recv, s_send, s_recv, r_send, r_recv, f_send, f_recv,
):
    dp = lax.axis_index("dp")
    row = lax.axis_index("row")
    z = lax.axis_index("col")
    y, core = dp // 2, dp % 2
    half, x = row // 4, row % 4

    def device(y=y, core=core, half=half, x=x, z=z):
        return {"dp": y * 2 + core, "row": half * 4 + x, "col": z}

    sibling = device(core=1 - core)
    ring = {"R": device(z=(z + 1) % 8), "L": device(z=(z + 7) % 8)}
    across = device(half=1 - half)
    y_peer = {1: device(y=y + 1 - 2 * (y % 2)), 2: device(y=(y + 2) % 4), 3: device(y=3 - y)}
    x_at = {m: (x + m) % 4 for m in (1, 2, 3)}
    x_peer = {m: device(x=x_at[m]) for m in (1, 2, 3)}

    def along_y(step):
        place = (half * 4 + y + step) % 8
        return device(y=place % 4, half=place // 4)

    pending = []
    waited = set()

    def send(src, dst, sems, index, to):
        copy = pltpu.make_async_remote_copy(
            src_ref=src, dst_ref=dst, send_sem=sems[0].at[index], recv_sem=sems[1].at[index],
            device_id=to, device_id_type=MESH,
        )
        copy.start()
        pending.append(copy)

    def arrived(dst, sems, index):
        if (id(sems), index) in waited:
            return
        waited.add((id(sems), index))
        pltpu.make_async_remote_copy(
            src_ref=dst, dst_ref=dst, send_sem=sems[0].at[index], recv_sem=sems[1].at[index],
            device_id=sibling, device_id_type=MESH,
        ).wait_recv()

    a_sem, j_sem, c_sem, z_sem = (a_send, a_recv), (j_send, j_recv), (c_send, c_recv), (z_send, z_recv)
    p_sem, y_sem, h_sem, s_sem = (p_send, p_recv), (y_send, y_recv), (h_send, h_recv), (s_send, s_recv)
    r_sem, f_sem = (r_send, r_recv), (f_send, f_recv)

    fetch = [
        pltpu.make_async_copy(tokens, TK.at[0], local_sem.at[0]),
        pltpu.make_async_copy(grad_out, TK.at[1], local_sem.at[1]),
        pltpu.make_async_copy(weight_in, WI, local_sem.at[2]),
        pltpu.make_async_copy(weight_out, WO, local_sem.at[3]),
    ]
    for copy in fetch:
        copy.start()

    barrier = pltpu.get_barrier_semaphore()
    peers = [sibling, *ring.values(), *y_peer.values(), *x_peer.values()]
    peers += [across]
    for peer in peers:
        pl.semaphore_signal(barrier, inc=1, device_id=peer, device_id_type=MESH)
    pl.semaphore_wait(barrier, len(peers))
    fetch[0].wait()
    fetch[1].wait()

    def do_a():
        for j in (1, 2, 3):
            send(TK.at[:, z], X.at[j, :, rows_of(0)], a_sem, j - 1, y_peer[j])

    def do_j():
        for r in range(8):
            for a in range(2):
                X[0, a, rows_of(PLACE[r])] = TK[a, (z + r) % 8]
        send(X.at[0, :, 0:128], X.at[0, :, 128:256], j_sem, 0, sibling)

    def z_index(j, s, d, a):
        return (((j - 1) * 4 + s) * 2 + "RL".index(d)) * 2 + a

    def z_arrays(s, d):
        return (0, 1) if s < 3 else (("RL".index(d)),)

    def z_arrived(j, s, d):
        place = PLACE[7 - s if d == "R" else s + 1]
        for a in z_arrays(s, d):
            arrived(X.at[j, a, rows_of(place)], z_sem, z_index(j, s, d, a))

    def do_z(j, s, d):
        if s == 0:
            arrived(X.at[j, :, rows_of(0)], a_sem, j - 1)
        place = PLACE[(8 - s) % 8 if d == "R" else s]
        to = PLACE[7 - s if d == "R" else s + 1]
        arrays = z_arrays(s, d)
        if s == 0:
            arrays = (0, 1) if d == "R" else (1, 0)
        for a in z_arrays(s - 1, d) if s else ():
            arrived(X.at[j, a, rows_of(PLACE[8 - s if d == "R" else s])], z_sem, z_index(j, s - 1, d, a))
            if a in arrays:
                send(X.at[j, a, rows_of(place)], X.at[j, a, rows_of(to)], z_sem, z_index(j, s, d, a), ring[d])
        if s == 0:
            for a in arrays:
                send(X.at[j, a, rows_of(place)], X.at[j, a, rows_of(to)], z_sem, z_index(j, s, d, a), ring[d])

    def do_s(j, s):
        z_arrived(j, s, "R")
        z_arrived(j, s, "L")
        q, n = STEP_PLACES[s]
        send(X.at[j, :, rows_of(q, n)], X.at[j, :, rows_of(8 + q, n)], c_sem, (j - 1) * 4 + s, sibling)

    def do_c(j):
        if j == 0:
            arrived(X.at[0, :, 128:256], j_sem, 0)
        else:
            for s in range(4):
                q, n = STEP_PLACES[s]
                arrived(X.at[j, :, rows_of(8 + q, n)], c_sem, (j - 1) * 4 + s)
        PS[:, j, 0] = times(X[j, 0], WI[...]).astype(BF16).reshape(4, 64, 384)
        for m in (2, 1, 3):
            send(PS.at[x_at[m], j, 0], PR.at[m - 1, j, 0], p_sem, j * 6 + m - 1, x_peer[m])
        PS[:, j, 1] = times_transposed(X[j, 1], WO[...]).astype(BF16).reshape(4, 64, 384)
        for m in (2, 1, 3):
            send(PS.at[x_at[m], j, 1], PR.at[m - 1, j, 1], p_sem, j * 6 + m + 2, x_peer[m])

    def do_d(j):
        for a in (0, 1):
            parts = (0, 1, 2)
            for m in (1, 2, 3):
                arrived(PR.at[m - 1, j, a], p_sem, j * 6 + a * 3 + m - 1)
            total = PS[x, j, a].astype(F32)
            for part in parts:
                total = total + PR[part, j, a].astype(F32)
            YS[j, a] = total.astype(BF16)
            send(YS.at[j, a], YR.at[j, a], y_sem, j * 4 + a, across)

    def h_index(j, d, second):
        return (j * 2 + "RL".index(d)) * 2 + second

    def do_e(j):
        for a in (0, 1):
            arrived(YR.at[j, a], y_sem, j * 4 + a)
        pre, grad = (YS[j, a].astype(F32) + YR[j, a].astype(F32) for a in (0, 1))
        value, slope = gelu_both(pre, grad)
        HC[j, 0, x] = value.astype(BF16)
        HC[j, 1, x] = slope.astype(BF16)
        for m in (2, 1, 3):
            send(HC.at[j, :, x], HC.at[j, :, x], h_sem, j * 4 + m, x_peer[m])

    def do_f(j):
        for m in (1, 2, 3):
            arrived(HC.at[j, :, x_at[4 - m]], h_sem, j * 4 + m)
        for a in (0, 1):
            lhs = HC[j, a].reshape(256, 384)
            val = times(lhs, WO[...]) if a == 0 else times_transposed(lhs, WI[...])
            OP[j, a] = val[0:128]
            SS[j, a] = val[128:256].astype(BF16)
        for part, (q, n) in enumerate(((5, 3), (0, 5))):
            send(SS.at[j, :, rows_of(q, n)], SR.at[j, :, rows_of(q, n)], s_sem, j * 2 + part, sibling)
        HT[:, j * 256:(j + 1) * 256] = HC[j, 0].reshape(256, 384).T
        GT[:, j * 256:(j + 1) * 256] = HC[j, 1].reshape(256, 384).T

    def r_index(j, i, d):
        return (j * 4 + i) * 2 + "RL".index(d)

    def r_ref(buffer, j, i, d):
        direction = "RL".index(d)
        if i == 0:
            return buffer.at[j, i, direction, direction]
        return buffer.at[j, i, direction]

    def both_cores(j, r, a):
        rows = rows_of(PLACE[r])
        return OP[j, a, rows] + SR[j, a, rows].astype(F32)

    def received(j, i, d, a):
        return ZR[j, i, "RL".index(d), a].astype(F32)

    def do_r(j, i, d):
        direction = "RL".index(d)
        q, n = ((5, 3), (0, 5))[i // 2]
        arrived(SR.at[j, :, rows_of(q, n)], s_sem, j * 2 + i // 2)
        r = 4 - i if d == "R" else 4 + i
        if i:
            arrived(r_ref(ZR, j, i - 1, d), r_sem, r_index(j, i - 1, d))
        for a in (0, 1) if i else (direction,):
            total = both_cores(j, r, a)
            if i > 1 or (i == 1 and a == direction):
                total = total + received(j, i - 1, d, a)
            ZS[j, i, direction, a] = total.astype(BF16)
        send(r_ref(ZS, j, i, d), r_ref(ZR, j, i, d), r_sem, r_index(j, i, d), ring[d])

    def do_h(j):
        arrived(SR.at[j, :, rows_of(0, 5)], s_sem, j * 2 + 1)
        for d in "RL":
            arrived(r_ref(ZR, j, 3, d), r_sem, r_index(j, 3, d))
        for a in (0, 1):
            total = both_cores(j, 0, a) + received(j, 3, "R", a) + received(j, 3, "L", a)
            if j == 0:
                FO[a] = total
            else:
                FS[j - 1, a] = total.astype(BF16)
        if j:
            send(FS.at[j - 1], FR.at[j - 1], f_sem, j - 1, y_peer[j])

    def do_w(k):
        cols = pl.ds(k * 256, min(256, 1152 - k * 256))
        GI[cols, :] = times(GT[...], X[:, 0, :, cols].reshape(1024, cols.size)).T.astype(BF16)
        GO[:, cols] = times(HT[...], X[:, 1, :, cols].reshape(1024, cols.size)).astype(BF16)

    def do_fin():
        stores = [
            pltpu.make_async_copy(GI, grad_weight_in, local_sem.at[4]),
            pltpu.make_async_copy(GO, grad_weight_out, local_sem.at[5]),
        ]
        for copy in stores:
            copy.start()
        total = FO[...]
        for j in (1, 2, 3):
            arrived(FR.at[j - 1], f_sem, j - 1)
            total = total + FR[j - 1].astype(F32)
        OB[...] = total.astype(BF16)
        stores.append(pltpu.make_async_copy(OB.at[0], layer_out, local_sem.at[6]))
        stores.append(pltpu.make_async_copy(OB.at[1], grad_tokens, local_sem.at[7]))
        stores[2].start()
        stores[3].start()
        for copy in pending:
            copy.wait_send()
        for copy in stores:
            copy.wait()

    steps = {
        "A": do_a, "J": do_j, "Z": do_z, "S": do_s, "C": do_c, "D": do_d, "E": do_e, "F": do_f,
        "R": do_r, "H": do_h, "W": do_w, "FIN": do_fin,
    }
    weights_here = False
    for step in ORDER:
        if step[0] == "C" and not weights_here:
            fetch[2].wait()
            fetch[3].wait()
            weights_here = True
        steps[step[0]](*step[1:])


def hand_out(*refs):
    copies = [
        pltpu.make_async_copy(refs[i], refs[4 + i], refs[8].at[i]) for i in (2, 3, 0, 1)
    ]
    for copy in copies:
        copy.start()
    for copy in copies:
        copy.wait()


def shards(tokens, weight_in, weight_out, grad_out):
    any_space = pl.BlockSpec(memory_space=pl.ANY)
    dma = pltpu.SemaphoreType.DMA
    shapes = (
        jax.ShapeDtypeStruct((16, 1152), BF16),
        jax.ShapeDtypeStruct((16, 1152), BF16),
        jax.ShapeDtypeStruct((1152, 384), BF16),
        jax.ShapeDtypeStruct((384, 1152), BF16),
    )
    results = pl.pallas_call(
        kernel,
        out_shape=shapes,
        in_specs=[any_space] * 4,
        out_specs=(any_space,) * 4,
        scratch_shapes=[
            pltpu.VMEM((2, 8, 16, 1152), BF16),
            pltpu.VMEM((4, 2, 256, 1152), BF16),
            pltpu.VMEM((1152, 384), BF16),
            pltpu.VMEM((384, 1152), BF16),
            pltpu.VMEM((4, 4, 2, 64, 384), BF16),
            pltpu.VMEM((3, 4, 2, 64, 384), BF16),
            pltpu.VMEM((4, 2, 64, 384), BF16),
            pltpu.VMEM((4, 2, 64, 384), BF16),
            pltpu.VMEM((4, 2, 4, 64, 384), BF16),
            pltpu.VMEM((384, 1024), BF16),
            pltpu.VMEM((384, 1024), BF16),
            pltpu.VMEM((4, 2, 128, 1152), BF16),
            pltpu.VMEM((4, 2, 128, 1152), BF16),
            pltpu.VMEM((4, 2, 128, 1152), F32),
            pltpu.VMEM((4, 4, 2, 2, 16, 1152), BF16),
            pltpu.VMEM((4, 4, 2, 2, 16, 1152), BF16),
            pltpu.VMEM((3, 2, 16, 1152), BF16),
            pltpu.VMEM((3, 2, 16, 1152), BF16),
            pltpu.VMEM((2, 16, 1152), F32),
            pltpu.VMEM((2, 16, 1152), BF16),
            pltpu.VMEM((1152, 384), BF16),
            pltpu.VMEM((384, 1152), BF16),
            pltpu.VMEM((4, 2, 64, 384), BF16),
            pltpu.VMEM((4, 2, 64, 384), BF16),
            pltpu.VMEM((4, 2, 64, 384), BF16),
            dma((8,)),
            dma((3,)), dma((3,)),
            dma((1,)), dma((1,)),
            dma((12,)), dma((12,)),
            dma((48,)), dma((48,)),
            dma((24,)), dma((24,)),
            dma((16,)), dma((16,)),
            dma((16,)), dma((16,)),
            dma((8,)), dma((8,)),
            dma((32,)), dma((32,)),
            dma((3,)), dma((3,)),
        ],
        compiler_params=pltpu.CompilerParams(
            collective_id=0, has_side_effects=True, vmem_limit_bytes=56 * 1024 * 1024
        ),
        cost_estimate=pl.CostEstimate(flops=5436000000, bytes_accessed=8000000, transcendentals=1000000),
    )(tokens.reshape(8, 16, 1152), weight_in, weight_out, grad_out.reshape(8, 16, 1152))
    return pl.pallas_call(
        hand_out,
        out_shape=shapes,
        in_specs=[any_space] * 4,
        out_specs=(any_space,) * 4,
        scratch_shapes=[dma((4,))],
    )(*results)


def solution(mesh):
    placed = (P("dp", "row"), P("row", ("dp", "col")), P(("dp", "col"), "row"), P("dp", "row"))
    return jax.shard_map(
        shards,
        mesh=mesh,
        in_specs=placed,
        out_specs=(
            P(("dp", "col"), "row"),
            P(("dp", "col"), "row"),
            P("row", ("dp", "col")),
            P(("dp", "col"), "row"),
        ),
        check_vma=False,
    )
```

time: 589 us -> 155 us (0.26)
  the two profiles are of different devices: /device:TPU:4 before, /device:TPU:64 now
where the time goes in v2:
time: 155 us
  Pallas kernels  154 us (99%)
    pallas_call x1, Pallas kernels, shards(): pl.pallas_call(kernel, out_shape=shapes, in_specs=[any_space] * 4, out_sp...  97 us
    pallas_call x1, Pallas kernels, shards(): pl.pallas_call(hand_out, out_shape=shapes, in_specs=[any_space] * 4, out_...  57 us

profile of v2, /device:TPU:64, one launch (start us, length us, event | category | flops | bytes accessed | tf_op | source)
XLA Modules:
  0.0 154.7 jit_solution(8639386848112972889)
XLA Ops:
  0.6 97.0 %shard_map.75 = (bf16[16,1152]{1,0:T(8,128)(2,1)}, bf16[16,1152]{1,0:T(8,128)(2,1)}, bf16[1152,384]{1,0:T(8,128)(2,1)}, bf16[384,1152]{1,0:T(8,128)(2,1)}) custom-call(bf16[8,16,1152]{2,1,0:T(8,128)(2,1)} %bitcast.2, bf16[1152,384]{1,0:T(8,128)(2,1)} %weight_in.1, bf16[384,1152]{1,0:T(8,128)(2,1)} %weight_out.1, bf16[8,16,1152]{2,1,0:T(8,128)(2,1)} %bitcast.3), custom_call_target="tpu_custom_call" | custom-call | flops 5436000256 | bytes 8000000 | tf_op jit(solution)/shard_map/pallas_call | solution.py:318
  97.7 57.0 %shard_map.76 = (bf16[16,1152]{1,0:T(8,128)(2,1)}, bf16[16,1152]{1,0:T(8,128)(2,1)}, bf16[1152,384]{1,0:T(8,128)(2,1)}, bf16[384,1152]{1,0:T(8,128)(2,1)}) custom-call(bf16[16,1152]{1,0:T(8,128)(2,1)} %get-tuple-element.8.refs_0_, bf16[16,1152]{1,0:T(8,128)(2,1)} %get-tuple-element.9.refs_1_, bf16[1152,384]{1,0:T(8,128)(2,1)} %get-tuple-element.10.refs_2_, ...), custom_call_target="tpu_custom_call" | custom-call | tf_op jit(solution)/shard_map/pallas_call | solution.py:366

commit v3 on v2

--- a/solution.py
+++ b/solution.py
@@ -14,19 +14,23 @@
 
 ORDER = (
     ("A",), ("J",), ("Z", 1, 0, "R"), ("Z", 1, 0, "L"), ("C", 0), ("Z", 1, 1, "R"), ("Z", 1, 1, "L"), ("S", 1, 0),
-    ("Z", 2, 0, "R"), ("Z", 2, 0, "L"), ("Z", 1, 2, "R"), ("Z", 1, 2, "L"), ("S", 1, 1), ("Z", 3, 0, "R"),
-    ("Z", 3, 0, "L"), ("D", 0), ("Z", 2, 1, "R"), ("Z", 2, 1, "L"), ("S", 2, 0), ("Z", 1, 3, "R"),
-    ("Z", 1, 3, "L"), ("S", 1, 2), ("Z", 3, 1, "R"), ("Z", 3, 1, "L"), ("S", 3, 0), ("Z", 2, 2, "R"), ("S", 2, 1),
-    ("Z", 2, 2, "L"), ("S", 1, 3), ("E", 0), ("Z", 3, 2, "R"), ("C", 1), ("Z", 3, 2, "L"), ("S", 3, 1),
-    ("Z", 2, 3, "R"), ("S", 2, 2), ("Z", 2, 3, "L"), ("Z", 3, 3, "R"), ("S", 3, 2), ("Z", 3, 3, "L"), ("S", 2, 3),
-    ("F", 0), ("S", 3, 3), ("C", 2), ("R", 0, 0, "R"), ("R", 0, 0, "L"), ("D", 1), ("C", 3), ("R", 0, 1, "R"),
-    ("R", 0, 1, "L"), ("D", 2), ("R", 0, 2, "R"), ("R", 0, 2, "L"), ("E", 1), ("R", 0, 3, "R"), ("R", 0, 3, "L"),
-    ("D", 3), ("H", 0), ("E", 2), ("F", 1), ("E", 3), ("R", 1, 0, "R"), ("R", 1, 0, "L"), ("F", 2),
-    ("R", 1, 1, "R"), ("R", 1, 1, "L"), ("R", 2, 0, "R"), ("R", 2, 0, "L"), ("F", 3), ("R", 2, 1, "R"),
-    ("R", 2, 1, "L"), ("W", 0), ("W", 1), ("R", 3, 0, "R"), ("R", 3, 0, "L"), ("W", 2), ("R", 2, 2, "R"),
-    ("R", 2, 2, "L"), ("W", 3), ("R", 3, 1, "R"), ("R", 3, 1, "L"), ("W", 4), ("R", 1, 2, "R"), ("R", 1, 2, "L"),
-    ("R", 2, 3, "R"), ("R", 2, 3, "L"), ("R", 3, 2, "R"), ("R", 3, 2, "L"), ("R", 1, 3, "R"), ("R", 1, 3, "L"),
-    ("H", 2), ("R", 3, 3, "R"), ("R", 3, 3, "L"), ("H", 1), ("H", 3), ("FIN",),
+    ("Z", 2, 0, "R"), ("Z", 2, 0, "L"), ("X2", 0, "R"), ("X2", 0, "L"), ("Z", 1, 2, "R"), ("Z", 1, 2, "L"),
+    ("S", 1, 1), ("D", 0), ("Z", 3, 0, "R"), ("Z", 3, 0, "L"), ("Z", 2, 1, "R"), ("Z", 2, 1, "L"), ("S", 2, 0),
+    ("Y2", 0, "p"), ("Z", 1, 3, "R"), ("Z", 1, 3, "L"), ("Y2", 0, "m"), ("S", 1, 2), ("Z", 3, 1, "R"),
+    ("Z", 3, 1, "L"), ("S", 3, 0), ("Z", 2, 2, "R"), ("S", 2, 1), ("Z", 2, 2, "L"), ("S", 1, 3), ("E", 0),
+    ("Z", 3, 2, "R"), ("Z", 3, 2, "L"), ("S", 3, 1), ("C", 1), ("Z", 2, 3, "R"), ("S", 2, 2), ("Z", 2, 3, "L"),
+    ("Z", 3, 3, "R"), ("S", 3, 2), ("Z", 3, 3, "L"), ("G2", 0, "R"), ("G2", 0, "L"), ("S", 2, 3), ("X2", 1, "R"),
+    ("X2", 1, "L"), ("S", 3, 3), ("C", 2), ("F", 0), ("D", 1), ("C", 3), ("X2", 2, "R"), ("X2", 2, "L"),
+    ("R", 0, 0, "R"), ("R", 0, 0, "L"), ("Y2", 1, "p"), ("Y2", 1, "m"), ("X2", 3, "R"), ("X2", 3, "L"),
+    ("R", 0, 1, "R"), ("R", 0, 1, "L"), ("D", 2), ("D", 3), ("R", 0, 2, "R"), ("R", 0, 2, "L"), ("E", 1),
+    ("Y2", 2, "p"), ("Y2", 2, "m"), ("Y2", 3, "p"), ("Y2", 3, "m"), ("R", 0, 3, "R"), ("R", 0, 3, "L"),
+    ("G2", 1, "R"), ("G2", 1, "L"), ("H", 0), ("E", 2), ("F", 1), ("E", 3), ("G2", 2, "R"), ("G2", 2, "L"),
+    ("R", 1, 0, "R"), ("R", 1, 0, "L"), ("R", 1, 1, "R"), ("R", 1, 1, "L"), ("G2", 3, "R"), ("G2", 3, "L"),
+    ("F", 2), ("R", 1, 2, "R"), ("R", 1, 2, "L"), ("F", 3), ("W", 0), ("R", 2, 0, "R"), ("R", 2, 0, "L"), ("W", 1),
+    ("R", 3, 0, "R"), ("R", 3, 0, "L"), ("R", 1, 3, "R"), ("R", 1, 3, "L"), ("W", 2), ("R", 2, 1, "R"),
+    ("R", 2, 1, "L"), ("W", 3), ("R", 3, 1, "R"), ("R", 3, 1, "L"), ("W", 4), ("H", 1), ("R", 2, 2, "R"),
+    ("R", 2, 2, "L"), ("R", 3, 2, "R"), ("R", 3, 2, "L"), ("R", 2, 3, "R"), ("R", 2, 3, "L"), ("R", 3, 3, "R"),
+    ("R", 3, 3, "L"), ("H", 2), ("H", 3), ("FIN",),
 )
 
 
@@ -113,7 +117,7 @@
 
     barrier = pltpu.get_barrier_semaphore()
     peers = [sibling, *ring.values(), *y_peer.values(), *x_peer.values()]
-    peers += [across]
+    peers += [along_y(step) for step in (1, 3, 5, 7)]
     for peer in peers:
         pl.semaphore_signal(barrier, inc=1, device_id=peer, device_id_type=MESH)
     pl.semaphore_wait(barrier, len(peers))
@@ -171,39 +175,55 @@
                 q, n = STEP_PLACES[s]
                 arrived(X.at[j, :, rows_of(8 + q, n)], c_sem, (j - 1) * 4 + s)
         PS[:, j, 0] = times(X[j, 0], WI[...]).astype(BF16).reshape(4, 64, 384)
-        for m in (2, 1, 3):
-            send(PS.at[x_at[m], j, 0], PR.at[m - 1, j, 0], p_sem, j * 6 + m - 1, x_peer[m])
+        send(PS.at[x_at[2], j, 0], XA.at[j, 0], p_sem, j * 6, x_peer[1])
+        send(PS.at[x_at[3], j, 0], PR.at[0, j, 0], p_sem, j * 6 + 1, x_peer[3])
         PS[:, j, 1] = times_transposed(X[j, 1], WO[...]).astype(BF16).reshape(4, 64, 384)
-        for m in (2, 1, 3):
-            send(PS.at[x_at[m], j, 1], PR.at[m - 1, j, 1], p_sem, j * 6 + m + 2, x_peer[m])
+        send(PS.at[x_at[2], j, 1], XA.at[j, 1], p_sem, j * 6 + 2, x_peer[3])
+        send(PS.at[x_at[1], j, 1], PR.at[0, j, 1], p_sem, j * 6 + 3, x_peer[1])
+
+    def do_x2(j, d):
+        a, m = (0, 1) if d == "R" else (1, 3)
+        arrived(XA.at[j, a], p_sem, j * 6 + a * 2)
+        XB[j, a] = (PS[x_at[m], j, a].astype(F32) + XA[j, a].astype(F32)).astype(BF16)
+        send(XB.at[j, a], PR.at[1, j, a], p_sem, j * 6 + 4 + a, x_peer[m])
 
     def do_d(j):
         for a in (0, 1):
-            parts = (0, 1, 2)
-            for m in (1, 2, 3):
-                arrived(PR.at[m - 1, j, a], p_sem, j * 6 + a * 3 + m - 1)
+            arrived(PR.at[0, j, a], p_sem, j * 6 + a * 2 + 1)
+            arrived(PR.at[1, j, a], p_sem, j * 6 + 4 + a)
+            parts = (0, 1)
             total = PS[x, j, a].astype(F32)
             for part in parts:
                 total = total + PR[part, j, a].astype(F32)
             YS[j, a] = total.astype(BF16)
-            send(YS.at[j, a], YR.at[j, a], y_sem, j * 4 + a, across)
+            send(YS.at[j, a], YT.at[j, a], y_sem, j * 4 + a, along_y((1, 7)[a]))
+
+    def do_y2(j, d):
+        a = "pm".index(d)
+        arrived(YT.at[j, a], y_sem, j * 4 + a)
+        send(YT.at[j, a], YR.at[j, a], y_sem, j * 4 + 2 + a, along_y((3, 5)[a]))
 
     def h_index(j, d, second):
         return (j * 2 + "RL".index(d)) * 2 + second
 
     def do_e(j):
         for a in (0, 1):
-            arrived(YR.at[j, a], y_sem, j * 4 + a)
+            arrived(YR.at[j, a], y_sem, j * 4 + 2 + a)
         pre, grad = (YS[j, a].astype(F32) + YR[j, a].astype(F32) for a in (0, 1))
         value, slope = gelu_both(pre, grad)
         HC[j, 0, x] = value.astype(BF16)
         HC[j, 1, x] = slope.astype(BF16)
-        for m in (2, 1, 3):
-            send(HC.at[j, :, x], HC.at[j, :, x], h_sem, j * 4 + m, x_peer[m])
+        for d, m in (("R", 1), ("L", 3)):
+            send(HC.at[j, :, x], HC.at[j, :, x], h_sem, h_index(j, d, 0), x_peer[m])
+
+    def do_g2(j, d):
+        m, a = (3, 0) if d == "R" else (1, 1)
+        arrived(HC.at[j, :, x_at[m]], h_sem, h_index(j, d, 0))
+        send(HC.at[j, a, x_at[m]], HC.at[j, a, x_at[m]], h_sem, h_index(j, d, 1), x_peer[4 - m])
 
     def do_f(j):
-        for m in (1, 2, 3):
-            arrived(HC.at[j, :, x_at[4 - m]], h_sem, j * 4 + m)
+        for a, d in ((0, "R"), (1, "L")):
+            arrived(HC.at[j, a, x_at[2]], h_sem, h_index(j, d, 1))
         for a in (0, 1):
             lhs = HC[j, a].reshape(256, 384)
             val = times(lhs, WO[...]) if a == 0 else times_transposed(lhs, WI[...])
@@ -287,6 +307,8 @@
         "A": do_a, "J": do_j, "Z": do_z, "S": do_s, "C": do_c, "D": do_d, "E": do_e, "F": do_f,
         "R": do_r, "H": do_h, "W": do_w, "FIN": do_fin,
     }
+    steps.update({"X2": do_x2, "G2": do_g2})
+    steps["Y2"] = do_y2
     weights_here = False
     for step in ORDER:
         if step[0] == "C" and not weights_here:
@@ -297,13 +319,17 @@
 
 
 def hand_out(*refs):
-    copies = [
-        pltpu.make_async_copy(refs[i], refs[4 + i], refs[8].at[i]) for i in (2, 3, 0, 1)
-    ]
-    for copy in copies:
-        copy.start()
-    for copy in copies:
-        copy.wait()
+    results, outputs, held, arrive, leave = refs[0:4], refs[4:8], refs[8:12], refs[12], refs[13]
+    order = (2, 3, 0, 1)
+    fetches = {i: pltpu.make_async_copy(results[i], held[i], arrive.at[i]) for i in order}
+    stores = {i: pltpu.make_async_copy(held[i], outputs[i], leave.at[i]) for i in order}
+    for i in order:
+        fetches[i].start()
+    for i in order:
+        fetches[i].wait()
+        stores[i].start()
+    for i in order:
+        stores[i].wait()
 
 
 def shards(tokens, weight_in, weight_out, grad_out):
@@ -368,7 +394,7 @@
         out_shape=shapes,
         in_specs=[any_space] * 4,
         out_specs=(any_space,) * 4,
-        scratch_shapes=[dma((4,))],
+        scratch_shapes=[*(pltpu.VMEM(shape.shape, BF16) for shape in shapes), dma((4,)), dma((4,))],
     )(*results)
 
 

time: 155 us -> 107 us (0.69)
  the two profiles are of different devices: /device:TPU:64 before, /device:TPU:8 now
where the time goes in v3:
time: 107 us
  Pallas kernels  106 us (99%)
    pallas_call x1, Pallas kernels, shards(): pl.pallas_call(kernel, out_shape=shapes, in_specs=[any_space] * 4, out_sp...  103 us
    pallas_call x1, Pallas kernels, shards(): pl.pallas_call(hand_out, out_shape=shapes, in_specs=[any_space] * 4, out_...  2.45 us

profile of v3, /device:TPU:8, one launch (start us, length us, event | category | flops | bytes accessed | tf_op | source)
XLA Modules:
  0.0 106.5 jit_solution(16165609068294045415)
XLA Ops:
  0.6 103.4 %shard_map.75 = (bf16[16,1152]{1,0:T(8,128)(2,1)}, bf16[16,1152]{1,0:T(8,128)(2,1)}, bf16[1152,384]{1,0:T(8,128)(2,1)}, bf16[384,1152]{1,0:T(8,128)(2,1)}) custom-call(bf16[8,16,1152]{2,1,0:T(8,128)(2,1)} %bitcast.2, bf16[1152,384]{1,0:T(8,128)(2,1)} %weight_in.1, bf16[384,1152]{1,0:T(8,128)(2,1)} %weight_out.1, bf16[8,16,1152]{2,1,0:T(8,128)(2,1)} %bitcast.3), custom_call_target="tpu_custom_call" | custom-call | flops 5436000256 | bytes 8000000 | tf_op jit(solution)/shard_map/pallas_call | solution.py:344
  104.1 2.4 %shard_map.76 = (bf16[16,1152]{1,0:T(8,128)(2,1)}, bf16[16,1152]{1,0:T(8,128)(2,1)}, bf16[1152,384]{1,0:T(8,128)(2,1)}, bf16[384,1152]{1,0:T(8,128)(2,1)}) custom-call(bf16[16,1152]{1,0:T(8,128)(2,1)} %get-tuple-element.8.refs_0_, bf16[16,1152]{1,0:T(8,128)(2,1)} %get-tuple-element.9.refs_1_, bf16[1152,384]{1,0:T(8,128)(2,1)} %get-tuple-element.10.refs_2_, ...), custom_call_target="tpu_custom_call" | custom-call | tf_op jit(solution)/shard_map/pallas_call | solution.py:392

commit v4 on v2

--- a/solution.py
+++ b/solution.py
@@ -10,23 +10,23 @@
 F32 = jnp.float32
 
 PLACE = {0: 0, 1: 1, 7: 2, 2: 3, 6: 4, 3: 5, 5: 6, 4: 7}
-STEP_PLACES = ((0, 3), (3, 2), (5, 2), (7, 1))
+STEPS_OF = ((0, 1), (2, 3))
+PLACES_OF = ((0, 5), (5, 3))
 
 ORDER = (
-    ("A",), ("J",), ("Z", 1, 0, "R"), ("Z", 1, 0, "L"), ("C", 0), ("Z", 1, 1, "R"), ("Z", 1, 1, "L"), ("S", 1, 0),
-    ("Z", 2, 0, "R"), ("Z", 2, 0, "L"), ("Z", 1, 2, "R"), ("Z", 1, 2, "L"), ("S", 1, 1), ("Z", 3, 0, "R"),
-    ("Z", 3, 0, "L"), ("D", 0), ("Z", 2, 1, "R"), ("Z", 2, 1, "L"), ("S", 2, 0), ("Z", 1, 3, "R"),
-    ("Z", 1, 3, "L"), ("S", 1, 2), ("Z", 3, 1, "R"), ("Z", 3, 1, "L"), ("S", 3, 0), ("Z", 2, 2, "R"), ("S", 2, 1),
-    ("Z", 2, 2, "L"), ("S", 1, 3), ("E", 0), ("Z", 3, 2, "R"), ("C", 1), ("Z", 3, 2, "L"), ("S", 3, 1),
-    ("Z", 2, 3, "R"), ("S", 2, 2), ("Z", 2, 3, "L"), ("Z", 3, 3, "R"), ("S", 3, 2), ("Z", 3, 3, "L"), ("S", 2, 3),
-    ("F", 0), ("S", 3, 3), ("C", 2), ("R", 0, 0, "R"), ("R", 0, 0, "L"), ("D", 1), ("C", 3), ("R", 0, 1, "R"),
-    ("R", 0, 1, "L"), ("D", 2), ("R", 0, 2, "R"), ("R", 0, 2, "L"), ("E", 1), ("R", 0, 3, "R"), ("R", 0, 3, "L"),
-    ("D", 3), ("H", 0), ("E", 2), ("F", 1), ("E", 3), ("R", 1, 0, "R"), ("R", 1, 0, "L"), ("F", 2),
-    ("R", 1, 1, "R"), ("R", 1, 1, "L"), ("R", 2, 0, "R"), ("R", 2, 0, "L"), ("F", 3), ("R", 2, 1, "R"),
-    ("R", 2, 1, "L"), ("W", 0), ("W", 1), ("R", 3, 0, "R"), ("R", 3, 0, "L"), ("W", 2), ("R", 2, 2, "R"),
-    ("R", 2, 2, "L"), ("W", 3), ("R", 3, 1, "R"), ("R", 3, 1, "L"), ("W", 4), ("R", 1, 2, "R"), ("R", 1, 2, "L"),
-    ("R", 2, 3, "R"), ("R", 2, 3, "L"), ("R", 3, 2, "R"), ("R", 3, 2, "L"), ("R", 1, 3, "R"), ("R", 1, 3, "L"),
-    ("H", 2), ("R", 3, 3, "R"), ("R", 3, 3, "L"), ("H", 1), ("H", 3), ("FIN",),
+    ("A",), ("J",), ("Z", 1, 0, "R"), ("Z", 1, 0, "L"), ("C", 0), ("Z", 2, 0, "R"), ("Z", 2, 0, "L"),
+    ("Z", 1, 1, "R"), ("Z", 1, 1, "L"), ("Z", 3, 0, "R"), ("Z", 3, 0, "L"), ("Z", 2, 1, "R"), ("Z", 2, 1, "L"),
+    ("Z", 1, 2, "R"), ("Z", 1, 2, "L"), ("S", 1, 0), ("D", 0), ("Z", 3, 1, "R"), ("Z", 3, 1, "L"),
+    ("Z", 2, 2, "R"), ("Z", 2, 2, "L"), ("S", 2, 0), ("Z", 1, 3, "R"), ("Z", 1, 3, "L"), ("Z", 3, 2, "R"),
+    ("Z", 3, 2, "L"), ("S", 3, 0), ("Z", 2, 3, "R"), ("Z", 2, 3, "L"), ("S", 1, 1), ("E", 0), ("Z", 3, 3, "R"),
+    ("Z", 3, 3, "L"), ("S", 2, 1), ("C", 1), ("S", 3, 1), ("C", 2), ("F", 0), ("C", 3), ("D", 1), ("R", 0, 0, "R"),
+    ("R", 0, 0, "L"), ("D", 2), ("R", 0, 1, "R"), ("R", 0, 1, "L"), ("D", 3), ("E", 1), ("R", 0, 2, "R"),
+    ("R", 0, 2, "L"), ("E", 2), ("R", 0, 3, "R"), ("R", 0, 3, "L"), ("E", 3), ("F", 1), ("H", 0), ("F", 2),
+    ("R", 1, 0, "R"), ("R", 1, 0, "L"), ("F", 3), ("R", 2, 0, "R"), ("R", 2, 0, "L"), ("R", 1, 1, "R"),
+    ("R", 1, 1, "L"), ("W", 0), ("R", 3, 0, "R"), ("R", 3, 0, "L"), ("R", 2, 1, "R"), ("R", 2, 1, "L"), ("W", 1),
+    ("R", 1, 2, "R"), ("R", 1, 2, "L"), ("R", 3, 1, "R"), ("R", 3, 1, "L"), ("W", 2), ("R", 2, 2, "R"),
+    ("R", 2, 2, "L"), ("W", 3), ("R", 1, 3, "R"), ("R", 1, 3, "L"), ("R", 3, 2, "R"), ("R", 3, 2, "L"), ("W", 4),
+    ("R", 2, 3, "R"), ("R", 2, 3, "L"), ("H", 1), ("R", 3, 3, "R"), ("R", 3, 3, "L"), ("H", 2), ("H", 3), ("FIN",),
 )
 
 
@@ -54,7 +54,7 @@
 def kernel(
     tokens, weight_in, weight_out, grad_out,
     layer_out, grad_tokens, grad_weight_in, grad_weight_out,
-    TK, X, WI, WO, PS, PR, YS, YR, HC, HT, GT, SS, SR, OP, ZS, ZR, FS, FR, FO, OB, GI, GO, XA, XB, YT,
+    TK, X, WI, WO, PS, PR, YS, YR, HC, HT, GT, SS, SR, OP, ZS, ZR, FS, FR, FO, OB, GI, GO,
     local_sem, a_send, a_recv, j_send, j_recv, c_send, c_recv, z_send, z_recv,
     p_send, p_recv, y_send, y_recv, h_send, h_recv, s_send, s_recv, r_send, r_recv, f_send, f_recv,
 ):
@@ -74,10 +74,6 @@
     x_at = {m: (x + m) % 4 for m in (1, 2, 3)}
     x_peer = {m: device(x=x_at[m]) for m in (1, 2, 3)}
 
-    def along_y(step):
-        place = (half * 4 + y + step) % 8
-        return device(y=place % 4, half=place // 4)
-
     pending = []
     waited = set()
 
@@ -130,70 +126,54 @@
                 X[0, a, rows_of(PLACE[r])] = TK[a, (z + r) % 8]
         send(X.at[0, :, 0:128], X.at[0, :, 128:256], j_sem, 0, sibling)
 
-    def z_index(j, s, d, a):
-        return (((j - 1) * 4 + s) * 2 + "RL".index(d)) * 2 + a
-
-    def z_arrays(s, d):
-        return (0, 1) if s < 3 else (("RL".index(d)),)
+    def z_piece(j, place, s, d):
+        rows = rows_of(place)
+        return X.at[j, :, rows] if s < 3 else X.at[j, "RL".index(d), rows]
+
+    def z_index(j, s, d):
+        return ((j - 1) * 4 + s) * 2 + "RL".index(d)
 
     def z_arrived(j, s, d):
         place = PLACE[7 - s if d == "R" else s + 1]
-        for a in z_arrays(s, d):
-            arrived(X.at[j, a, rows_of(place)], z_sem, z_index(j, s, d, a))
+        arrived(z_piece(j, place, s, d), z_sem, z_index(j, s, d))
 
     def do_z(j, s, d):
         if s == 0:
             arrived(X.at[j, :, rows_of(0)], a_sem, j - 1)
+        else:
+            z_arrived(j, s - 1, d)
         place = PLACE[(8 - s) % 8 if d == "R" else s]
         to = PLACE[7 - s if d == "R" else s + 1]
-        arrays = z_arrays(s, d)
-        if s == 0:
-            arrays = (0, 1) if d == "R" else (1, 0)
-        for a in z_arrays(s - 1, d) if s else ():
-            arrived(X.at[j, a, rows_of(PLACE[8 - s if d == "R" else s])], z_sem, z_index(j, s - 1, d, a))
-            if a in arrays:
-                send(X.at[j, a, rows_of(place)], X.at[j, a, rows_of(to)], z_sem, z_index(j, s, d, a), ring[d])
-        if s == 0:
-            for a in arrays:
-                send(X.at[j, a, rows_of(place)], X.at[j, a, rows_of(to)], z_sem, z_index(j, s, d, a), ring[d])
-
-    def do_s(j, s):
-        z_arrived(j, s, "R")
-        z_arrived(j, s, "L")
-        q, n = STEP_PLACES[s]
-        send(X.at[j, :, rows_of(q, n)], X.at[j, :, rows_of(8 + q, n)], c_sem, (j - 1) * 4 + s, sibling)
+        send(z_piece(j, place, s, d), z_piece(j, to, s, d), z_sem, z_index(j, s, d), ring[d])
+
+    def do_s(j, part):
+        for s in STEPS_OF[part]:
+            z_arrived(j, s, "R")
+            z_arrived(j, s, "L")
+        q, n = PLACES_OF[part]
+        send(X.at[j, :, rows_of(q, n)], X.at[j, :, rows_of(8 + q, n)], c_sem, (j - 1) * 2 + part, sibling)
 
     def do_c(j):
         if j == 0:
             arrived(X.at[0, :, 128:256], j_sem, 0)
         else:
-            for s in range(4):
-                q, n = STEP_PLACES[s]
-                arrived(X.at[j, :, rows_of(8 + q, n)], c_sem, (j - 1) * 4 + s)
+            for part, (q, n) in enumerate(PLACES_OF):
+                arrived(X.at[j, :, rows_of(8 + q, n)], c_sem, (j - 1) * 2 + part)
         PS[:, j, 0] = times(X[j, 0], WI[...]).astype(BF16).reshape(4, 64, 384)
-        for m in (2, 1, 3):
-            send(PS.at[x_at[m], j, 0], PR.at[m - 1, j, 0], p_sem, j * 6 + m - 1, x_peer[m])
         PS[:, j, 1] = times_transposed(X[j, 1], WO[...]).astype(BF16).reshape(4, 64, 384)
         for m in (2, 1, 3):
-            send(PS.at[x_at[m], j, 1], PR.at[m - 1, j, 1], p_sem, j * 6 + m + 2, x_peer[m])
+            send(PS.at[x_at[m], j], PR.at[m - 1, j], p_sem, j * 3 + m - 1, x_peer[m])
 
     def do_d(j):
-        for a in (0, 1):
-            parts = (0, 1, 2)
-            for m in (1, 2, 3):
-                arrived(PR.at[m - 1, j, a], p_sem, j * 6 + a * 3 + m - 1)
-            total = PS[x, j, a].astype(F32)
-            for part in parts:
-                total = total + PR[part, j, a].astype(F32)
-            YS[j, a] = total.astype(BF16)
-            send(YS.at[j, a], YR.at[j, a], y_sem, j * 4 + a, across)
-
-    def h_index(j, d, second):
-        return (j * 2 + "RL".index(d)) * 2 + second
+        total = PS[x, j].astype(F32)
+        for m in (1, 2, 3):
+            arrived(PR.at[m - 1, j], p_sem, j * 3 + m - 1)
+            total = total + PR[m - 1, j].astype(F32)
+        YS[j] = total.astype(BF16)
+        send(YS.at[j], YR.at[j], y_sem, j, across)
 
     def do_e(j):
-        for a in (0, 1):
-            arrived(YR.at[j, a], y_sem, j * 4 + a)
+        arrived(YR.at[j], y_sem, j)
         pre, grad = (YS[j, a].astype(F32) + YR[j, a].astype(F32) for a in (0, 1))
         value, slope = gelu_both(pre, grad)
         HC[j, 0, x] = value.astype(BF16)
@@ -294,16 +274,22 @@
             fetch[3].wait()
             weights_here = True
         steps[step[0]](*step[1:])
+        while len(pending) > 24:
+            pending.pop(0).wait_send()
 
 
 def hand_out(*refs):
-    copies = [
-        pltpu.make_async_copy(refs[i], refs[4 + i], refs[8].at[i]) for i in (2, 3, 0, 1)
-    ]
-    for copy in copies:
-        copy.start()
-    for copy in copies:
-        copy.wait()
+    results, outputs, held, arrive, leave = refs[0:4], refs[4:8], refs[8:12], refs[12], refs[13]
+    order = (2, 3, 0, 1)
+    fetches = {i: pltpu.make_async_copy(results[i], held[i], arrive.at[i]) for i in order}
+    stores = {i: pltpu.make_async_copy(held[i], outputs[i], leave.at[i]) for i in order}
+    for i in order:
+        fetches[i].start()
+    for i in order:
+        fetches[i].wait()
+        stores[i].start()
+    for i in order:
+        stores[i].wait()
 
 
 def shards(tokens, weight_in, weight_out, grad_out):
@@ -343,16 +329,13 @@
             pltpu.VMEM((2, 16, 1152), BF16),
             pltpu.VMEM((1152, 384), BF16),
             pltpu.VMEM((384, 1152), BF16),
-            pltpu.VMEM((4, 2, 64, 384), BF16),
-            pltpu.VMEM((4, 2, 64, 384), BF16),
-            pltpu.VMEM((4, 2, 64, 384), BF16),
             dma((8,)),
             dma((3,)), dma((3,)),
             dma((1,)), dma((1,)),
+            dma((6,)), dma((6,)),
+            dma((24,)), dma((24,)),
             dma((12,)), dma((12,)),
-            dma((48,)), dma((48,)),
-            dma((24,)), dma((24,)),
-            dma((16,)), dma((16,)),
+            dma((4,)), dma((4,)),
             dma((16,)), dma((16,)),
             dma((8,)), dma((8,)),
             dma((32,)), dma((32,)),
@@ -368,7 +351,7 @@
         out_shape=shapes,
         in_specs=[any_space] * 4,
         out_specs=(any_space,) * 4,
-        scratch_shapes=[dma((4,))],
+        scratch_shapes=[*(pltpu.VMEM(shape.shape, BF16) for shape in shapes), dma((4,)), dma((4,))],
     )(*results)
 
 

time: 155 us -> 99.4 us (0.64)
  the two profiles are of different devices: /device:TPU:64 before, /device:TPU:58 now
where the time goes in v4:
time: 99.4 us; the launch traced here: 99.2 us
  Pallas kernels  98.6 us (99%)
    pallas_call x1, Pallas kernels, shards(): pl.pallas_call(kernel, out_shape=shapes, in_specs=[any_space] * 4, out_sp...  96.1 us
    pallas_call x1, Pallas kernels, shards(): pl.pallas_call(hand_out, out_shape=shapes, in_specs=[any_space] * 4, out_...  2.45 us

profile of v4, /device:TPU:58, one launch (start us, length us, event | category | flops | bytes accessed | tf_op | source)
XLA Modules:
  0.0 99.2 jit_solution(16171546324656478178)
XLA Ops:
  0.6 96.1 %shard_map.75 = (bf16[16,1152]{1,0:T(8,128)(2,1)}, bf16[16,1152]{1,0:T(8,128)(2,1)}, bf16[1152,384]{1,0:T(8,128)(2,1)}, bf16[384,1152]{1,0:T(8,128)(2,1)}) custom-call(bf16[8,16,1152]{2,1,0:T(8,128)(2,1)} %bitcast.2, bf16[1152,384]{1,0:T(8,128)(2,1)} %weight_in.1, bf16[384,1152]{1,0:T(8,128)(2,1)} %weight_out.1, bf16[8,16,1152]{2,1,0:T(8,128)(2,1)} %bitcast.3), custom_call_target="tpu_custom_call" | custom-call | flops 5436000256 | bytes 8000000 | tf_op jit(solution)/shard_map/pallas_call | solution.py:304
  96.8 2.4 %shard_map.76 = (bf16[16,1152]{1,0:T(8,128)(2,1)}, bf16[16,1152]{1,0:T(8,128)(2,1)}, bf16[1152,384]{1,0:T(8,128)(2,1)}, bf16[384,1152]{1,0:T(8,128)(2,1)}) custom-call(bf16[16,1152]{1,0:T(8,128)(2,1)} %get-tuple-element.8.refs_0_, bf16[16,1152]{1,0:T(8,128)(2,1)} %get-tuple-element.9.refs_1_, bf16[1152,384]{1,0:T(8,128)(2,1)} %get-tuple-element.10.refs_2_, ...), custom_call_target="tpu_custom_call" | custom-call | tf_op jit(solution)/shard_map/pallas_call | solution.py:349

commit v5 on v4

--- a/solution.py
+++ b/solution.py
@@ -14,19 +14,19 @@
 PLACES_OF = ((0, 5), (5, 3))
 
 ORDER = (
-    ("A",), ("J",), ("Z", 1, 0, "R"), ("Z", 1, 0, "L"), ("C", 0), ("Z", 2, 0, "R"), ("Z", 2, 0, "L"),
-    ("Z", 1, 1, "R"), ("Z", 1, 1, "L"), ("Z", 3, 0, "R"), ("Z", 3, 0, "L"), ("Z", 2, 1, "R"), ("Z", 2, 1, "L"),
-    ("Z", 1, 2, "R"), ("Z", 1, 2, "L"), ("S", 1, 0), ("D", 0), ("Z", 3, 1, "R"), ("Z", 3, 1, "L"),
-    ("Z", 2, 2, "R"), ("Z", 2, 2, "L"), ("S", 2, 0), ("Z", 1, 3, "R"), ("Z", 1, 3, "L"), ("Z", 3, 2, "R"),
-    ("Z", 3, 2, "L"), ("S", 3, 0), ("Z", 2, 3, "R"), ("Z", 2, 3, "L"), ("S", 1, 1), ("E", 0), ("Z", 3, 3, "R"),
-    ("Z", 3, 3, "L"), ("S", 2, 1), ("C", 1), ("S", 3, 1), ("C", 2), ("F", 0), ("C", 3), ("D", 1), ("R", 0, 0, "R"),
-    ("R", 0, 0, "L"), ("D", 2), ("R", 0, 1, "R"), ("R", 0, 1, "L"), ("D", 3), ("E", 1), ("R", 0, 2, "R"),
-    ("R", 0, 2, "L"), ("E", 2), ("R", 0, 3, "R"), ("R", 0, 3, "L"), ("E", 3), ("F", 1), ("H", 0), ("F", 2),
-    ("R", 1, 0, "R"), ("R", 1, 0, "L"), ("F", 3), ("R", 2, 0, "R"), ("R", 2, 0, "L"), ("R", 1, 1, "R"),
-    ("R", 1, 1, "L"), ("W", 0), ("R", 3, 0, "R"), ("R", 3, 0, "L"), ("R", 2, 1, "R"), ("R", 2, 1, "L"), ("W", 1),
-    ("R", 1, 2, "R"), ("R", 1, 2, "L"), ("R", 3, 1, "R"), ("R", 3, 1, "L"), ("W", 2), ("R", 2, 2, "R"),
-    ("R", 2, 2, "L"), ("W", 3), ("R", 1, 3, "R"), ("R", 1, 3, "L"), ("R", 3, 2, "R"), ("R", 3, 2, "L"), ("W", 4),
-    ("R", 2, 3, "R"), ("R", 2, 3, "L"), ("H", 1), ("R", 3, 3, "R"), ("R", 3, 3, "L"), ("H", 2), ("H", 3), ("FIN",),
+    ("A",), ("J",), ("Z", 1, 0, "R"), ("Z", 1, 0, "L"), ("Z", 2, 0, "R"), ("Z", 2, 0, "L"), ("Z", 1, 1, "R"),
+    ("Z", 1, 1, "L"), ("C", 0), ("Z", 3, 0, "R"), ("Z", 3, 0, "L"), ("Z", 2, 1, "R"), ("Z", 2, 1, "L"),
+    ("Z", 1, 2, "R"), ("S", 1, 0), ("Z", 1, 2, "L"), ("Z", 3, 1, "R"), ("Z", 3, 1, "L"), ("Z", 2, 2, "R"),
+    ("S", 2, 0), ("Z", 2, 2, "L"), ("Z", 1, 3, "R"), ("Z", 1, 3, "L"), ("D", 0), ("Z", 3, 2, "R"), ("S", 3, 0),
+    ("Z", 3, 2, "L"), ("Z", 2, 3, "R"), ("Z", 2, 3, "L"), ("S", 1, 1), ("Z", 3, 3, "R"), ("Z", 3, 3, "L"),
+    ("S", 2, 1), ("S", 3, 1), ("C", 1), ("C", 2), ("C", 3), ("E", 0), ("D", 1), ("D", 2), ("E", 1), ("D", 3),
+    ("F", 0), ("E", 2), ("F", 1), ("R", 0, 0, "R"), ("E", 3), ("R", 0, 0, "L"), ("R", 0, 1, "R"), ("F", 2),
+    ("R", 0, 1, "L"), ("R", 1, 0, "R"), ("R", 0, 2, "R"), ("R", 1, 0, "L"), ("R", 1, 1, "R"), ("R", 0, 2, "L"),
+    ("F", 3), ("R", 2, 0, "R"), ("R", 0, 3, "R"), ("R", 2, 0, "L"), ("R", 0, 3, "L"), ("R", 1, 1, "L"),
+    ("R", 1, 2, "R"), ("W", 0), ("R", 2, 1, "R"), ("R", 2, 1, "L"), ("W", 1), ("R", 3, 0, "R"), ("H", 0),
+    ("R", 1, 3, "R"), ("R", 1, 2, "L"), ("R", 3, 0, "L"), ("R", 2, 2, "R"), ("W", 2), ("R", 3, 1, "R"),
+    ("R", 2, 2, "L"), ("W", 3), ("R", 3, 1, "L"), ("R", 2, 3, "R"), ("R", 1, 3, "L"), ("W", 4), ("R", 3, 2, "R"),
+    ("R", 2, 3, "L"), ("R", 3, 2, "L"), ("H", 1), ("R", 3, 3, "R"), ("H", 2), ("R", 3, 3, "L"), ("H", 3), ("FIN",),
 )
 
 
@@ -74,30 +74,39 @@
     x_at = {m: (x + m) % 4 for m in (1, 2, 3)}
     x_peer = {m: device(x=x_at[m]) for m in (1, 2, 3)}
 
-    pending = []
     waited = set()
 
     def send(src, dst, sems, index, to):
         copy = pltpu.make_async_remote_copy(
-            src_ref=src, dst_ref=dst, send_sem=sems[0].at[index], recv_sem=sems[1].at[index],
+            src_ref=src, dst_ref=dst, send_sem=sems[0], recv_sem=sems[1].at[index],
             device_id=to, device_id_type=MESH,
         )
         copy.start()
-        pending.append(copy)
 
     def arrived(dst, sems, index):
         if (id(sems), index) in waited:
             return
         waited.add((id(sems), index))
         pltpu.make_async_remote_copy(
-            src_ref=dst, dst_ref=dst, send_sem=sems[0].at[index], recv_sem=sems[1].at[index],
+            src_ref=dst, dst_ref=dst, send_sem=sems[0], recv_sem=sems[1].at[index],
             device_id=sibling, device_id_type=MESH,
         ).wait_recv()
+
+    def all_left(ref, sems):
+        pltpu.make_async_remote_copy(
+            src_ref=ref, dst_ref=ref, send_sem=sems[0], recv_sem=sems[1].at[0],
+            device_id=sibling, device_id_type=MESH,
+        ).wait_send()
 
     a_sem, j_sem, c_sem, z_sem = (a_send, a_recv), (j_send, j_recv), (c_send, c_recv), (z_send, z_recv)
     p_sem, y_sem, h_sem, s_sem = (p_send, p_recv), (y_send, y_recv), (h_send, h_recv), (s_send, s_recv)
     r_sem, f_sem = (r_send, r_recv), (f_send, f_recv)
 
+    barrier = pltpu.get_barrier_semaphore()
+    peers = [sibling, *ring.values(), *y_peer.values(), *x_peer.values()]
+    peers += [across]
+    for peer in peers:
+        pl.semaphore_signal(barrier, inc=1, device_id=peer, device_id_type=MESH)
     fetch = [
         pltpu.make_async_copy(tokens, TK.at[0], local_sem.at[0]),
         pltpu.make_async_copy(grad_out, TK.at[1], local_sem.at[1]),
@@ -107,11 +116,6 @@
     for copy in fetch:
         copy.start()
 
-    barrier = pltpu.get_barrier_semaphore()
-    peers = [sibling, *ring.values(), *y_peer.values(), *x_peer.values()]
-    peers += [across]
-    for peer in peers:
-        pl.semaphore_signal(barrier, inc=1, device_id=peer, device_id_type=MESH)
     pl.semaphore_wait(barrier, len(peers))
     fetch[0].wait()
     fetch[1].wait()
@@ -151,23 +155,22 @@
             z_arrived(j, s, "R")
             z_arrived(j, s, "L")
         q, n = PLACES_OF[part]
-        send(X.at[j, :, rows_of(q, n)], X.at[j, :, rows_of(8 + q, n)], c_sem, (j - 1) * 2 + part, sibling)
+        send(X.at[j, :, rows_of(q, n)], X.at[j, :, rows_of(8 + q, n)], c_sem, j - 1, sibling)
 
     def do_c(j):
         if j == 0:
             arrived(X.at[0, :, 128:256], j_sem, 0)
         else:
-            for part, (q, n) in enumerate(PLACES_OF):
-                arrived(X.at[j, :, rows_of(8 + q, n)], c_sem, (j - 1) * 2 + part)
+            arrived(X.at[j, :, 128:256], c_sem, j - 1)
         PS[:, j, 0] = times(X[j, 0], WI[...]).astype(BF16).reshape(4, 64, 384)
         PS[:, j, 1] = times_transposed(X[j, 1], WO[...]).astype(BF16).reshape(4, 64, 384)
         for m in (2, 1, 3):
-            send(PS.at[x_at[m], j], PR.at[m - 1, j], p_sem, j * 3 + m - 1, x_peer[m])
+            send(PS.at[x_at[m], j], PR.at[m - 1, j], p_sem, j, x_peer[m])
 
     def do_d(j):
+        arrived(PR.at[:, j], p_sem, j)
         total = PS[x, j].astype(F32)
         for m in (1, 2, 3):
-            arrived(PR.at[m - 1, j], p_sem, j * 3 + m - 1)
             total = total + PR[m - 1, j].astype(F32)
         YS[j] = total.astype(BF16)
         send(YS.at[j], YR.at[j], y_sem, j, across)
@@ -179,18 +182,16 @@
         HC[j, 0, x] = value.astype(BF16)
         HC[j, 1, x] = slope.astype(BF16)
         for m in (2, 1, 3):
-            send(HC.at[j, :, x], HC.at[j, :, x], h_sem, j * 4 + m, x_peer[m])
+            send(HC.at[j, :, x], HC.at[j, :, x], h_sem, j, x_peer[m])
 
     def do_f(j):
-        for m in (1, 2, 3):
-            arrived(HC.at[j, :, x_at[4 - m]], h_sem, j * 4 + m)
+        arrived(PR.at[:, j], h_sem, j)
         for a in (0, 1):
             lhs = HC[j, a].reshape(256, 384)
             val = times(lhs, WO[...]) if a == 0 else times_transposed(lhs, WI[...])
             OP[j, a] = val[0:128]
             SS[j, a] = val[128:256].astype(BF16)
-        for part, (q, n) in enumerate(((5, 3), (0, 5))):
-            send(SS.at[j, :, rows_of(q, n)], SR.at[j, :, rows_of(q, n)], s_sem, j * 2 + part, sibling)
+            send(SS.at[j, a], SR.at[j, a], s_sem, j * 2 + a, sibling)
         HT[:, j * 256:(j + 1) * 256] = HC[j, 0].reshape(256, 384).T
         GT[:, j * 256:(j + 1) * 256] = HC[j, 1].reshape(256, 384).T
 
@@ -212,8 +213,8 @@
 
     def do_r(j, i, d):
         direction = "RL".index(d)
-        q, n = ((5, 3), (0, 5))[i // 2]
-        arrived(SR.at[j, :, rows_of(q, n)], s_sem, j * 2 + i // 2)
+        for a in (0, 1) if i else (direction,):
+            arrived(SR.at[j, a], s_sem, j * 2 + a)
         r = 4 - i if d == "R" else 4 + i
         if i:
             arrived(r_ref(ZR, j, i - 1, d), r_sem, r_index(j, i - 1, d))
@@ -225,7 +226,8 @@
         send(r_ref(ZS, j, i, d), r_ref(ZR, j, i, d), r_sem, r_index(j, i, d), ring[d])
 
     def do_h(j):
-        arrived(SR.at[j, :, rows_of(0, 5)], s_sem, j * 2 + 1)
+        for a in (0, 1):
+            arrived(SR.at[j, a], s_sem, j * 2 + a)
         for d in "RL":
             arrived(r_ref(ZR, j, 3, d), r_sem, r_index(j, 3, d))
         for a in (0, 1):
@@ -258,8 +260,16 @@
         stores.append(pltpu.make_async_copy(OB.at[1], grad_tokens, local_sem.at[7]))
         stores[2].start()
         stores[3].start()
-        for copy in pending:
-            copy.wait_send()
+        all_left(FS, a_sem)
+        all_left(X.at[0, :, 0:128], j_sem)
+        all_left(X.at[1:4, :, 0:128], c_sem)
+        all_left(X.at[1:4, :, 0:112], z_sem)
+        all_left(PR, p_sem)
+        all_left(YS, y_sem)
+        all_left(PR, h_sem)
+        all_left(SS, s_sem)
+        all_left(X.at[:, :, 0:112], r_sem)
+        all_left(FS, f_sem)
         for copy in stores:
             copy.wait()
 
@@ -274,8 +284,6 @@
             fetch[3].wait()
             weights_here = True
         steps[step[0]](*step[1:])
-        while len(pending) > 24:
-            pending.pop(0).wait_send()
 
 
 def hand_out(*refs):
@@ -330,16 +338,16 @@
             pltpu.VMEM((1152, 384), BF16),
             pltpu.VMEM((384, 1152), BF16),
             dma((8,)),
-            dma((3,)), dma((3,)),
-            dma((1,)), dma((1,)),
-            dma((6,)), dma((6,)),
-            dma((24,)), dma((24,)),
-            dma((12,)), dma((12,)),
-            dma((4,)), dma((4,)),
-            dma((16,)), dma((16,)),
-            dma((8,)), dma((8,)),
-            dma((32,)), dma((32,)),
-            dma((3,)), dma((3,)),
+            dma, dma((3,)),
+            dma, dma((1,)),
+            dma, dma((3,)),
+            dma, dma((24,)),
+            dma, dma((4,)),
+            dma, dma((4,)),
+            dma, dma((4,)),
+            dma, dma((8,)),
+            dma, dma((32,)),
+            dma, dma((3,)),
         ],
         compiler_params=pltpu.CompilerParams(
             collective_id=0, has_side_effects=True, vmem_limit_bytes=56 * 1024 * 1024

time: 99.4 us -> 108 us (1.087)
  the two profiles are of different devices: /device:TPU:58 before, /device:TPU:24 now
where the time goes in v5:
time: 108 us
  Pallas kernels  107 us (99%)
    pallas_call x1, Pallas kernels, shards(): pl.pallas_call(kernel, out_shape=shapes, in_specs=[any_space] * 4, out_sp...  105 us
    pallas_call x1, Pallas kernels, shards(): pl.pallas_call(hand_out, out_shape=shapes, in_specs=[any_space] * 4, out_...  2.45 us

profile of v5, /device:TPU:24, one launch (start us, length us, event | category | flops | bytes accessed | tf_op | source)
XLA Modules:
  0.0 107.6 jit_solution(10760744614812558008)
XLA Ops:
  0.6 104.6 %shard_map.75 = (bf16[16,1152]{1,0:T(8,128)(2,1)}, bf16[16,1152]{1,0:T(8,128)(2,1)}, bf16[1152,384]{1,0:T(8,128)(2,1)}, bf16[384,1152]{1,0:T(8,128)(2,1)}) custom-call(bf16[8,16,1152]{2,1,0:T(8,128)(2,1)} %bitcast.2, bf16[1152,384]{1,0:T(8,128)(2,1)} %weight_in.1, bf16[384,1152]{1,0:T(8,128)(2,1)} %weight_out.1, bf16[8,16,1152]{2,1,0:T(8,128)(2,1)} %bitcast.3), custom_call_target="tpu_custom_call" | custom-call | flops 5436000256 | bytes 8000000 | tf_op jit(solution)/shard_map/pallas_call | solution.py:312
  105.2 2.4 %shard_map.76 = (bf16[16,1152]{1,0:T(8,128)(2,1)}, bf16[16,1152]{1,0:T(8,128)(2,1)}, bf16[1152,384]{1,0:T(8,128)(2,1)}, bf16[384,1152]{1,0:T(8,128)(2,1)}) custom-call(bf16[16,1152]{1,0:T(8,128)(2,1)} %get-tuple-element.8.refs_0_, bf16[16,1152]{1,0:T(8,128)(2,1)} %get-tuple-element.9.refs_1_, bf16[1152,384]{1,0:T(8,128)(2,1)} %get-tuple-element.10.refs_2_, ...), custom_call_target="tpu_custom_call" | custom-call | tf_op jit(solution)/shard_map/pallas_call | solution.py:357

commit v6 on v5

--- a/solution.py
+++ b/solution.py
@@ -9,24 +9,19 @@
 BF16 = jnp.bfloat16
 F32 = jnp.float32
 
-PLACE = {0: 0, 1: 1, 7: 2, 2: 3, 6: 4, 3: 5, 5: 6, 4: 7}
-STEPS_OF = ((0, 1), (2, 3))
-PLACES_OF = ((0, 5), (5, 3))
-
+PLACE = {0: 0, 4: 1, 7: 2, 3: 3, 1: 4, 5: 5, 2: 6, 6: 7}
 ORDER = (
-    ("A",), ("J",), ("Z", 1, 0, "R"), ("Z", 1, 0, "L"), ("Z", 2, 0, "R"), ("Z", 2, 0, "L"), ("Z", 1, 1, "R"),
-    ("Z", 1, 1, "L"), ("C", 0), ("Z", 3, 0, "R"), ("Z", 3, 0, "L"), ("Z", 2, 1, "R"), ("Z", 2, 1, "L"),
-    ("Z", 1, 2, "R"), ("S", 1, 0), ("Z", 1, 2, "L"), ("Z", 3, 1, "R"), ("Z", 3, 1, "L"), ("Z", 2, 2, "R"),
-    ("S", 2, 0), ("Z", 2, 2, "L"), ("Z", 1, 3, "R"), ("Z", 1, 3, "L"), ("D", 0), ("Z", 3, 2, "R"), ("S", 3, 0),
-    ("Z", 3, 2, "L"), ("Z", 2, 3, "R"), ("Z", 2, 3, "L"), ("S", 1, 1), ("Z", 3, 3, "R"), ("Z", 3, 3, "L"),
-    ("S", 2, 1), ("S", 3, 1), ("C", 1), ("C", 2), ("C", 3), ("E", 0), ("D", 1), ("D", 2), ("E", 1), ("D", 3),
-    ("F", 0), ("E", 2), ("F", 1), ("R", 0, 0, "R"), ("E", 3), ("R", 0, 0, "L"), ("R", 0, 1, "R"), ("F", 2),
-    ("R", 0, 1, "L"), ("R", 1, 0, "R"), ("R", 0, 2, "R"), ("R", 1, 0, "L"), ("R", 1, 1, "R"), ("R", 0, 2, "L"),
-    ("F", 3), ("R", 2, 0, "R"), ("R", 0, 3, "R"), ("R", 2, 0, "L"), ("R", 0, 3, "L"), ("R", 1, 1, "L"),
-    ("R", 1, 2, "R"), ("W", 0), ("R", 2, 1, "R"), ("R", 2, 1, "L"), ("W", 1), ("R", 3, 0, "R"), ("H", 0),
-    ("R", 1, 3, "R"), ("R", 1, 2, "L"), ("R", 3, 0, "L"), ("R", 2, 2, "R"), ("W", 2), ("R", 3, 1, "R"),
-    ("R", 2, 2, "L"), ("W", 3), ("R", 3, 1, "L"), ("R", 2, 3, "R"), ("R", 1, 3, "L"), ("W", 4), ("R", 3, 2, "R"),
-    ("R", 2, 3, "L"), ("R", 3, 2, "L"), ("H", 1), ("R", 3, 3, "R"), ("H", 2), ("R", 3, 3, "L"), ("H", 3), ("FIN",),
+    ("A",), ("J",), ("Z", 1, 0, "R"), ("Z", 1, 0, "L"), ("C", 0), ("Z", 1, 1, "R"), ("Z", 1, 1, "L"), ("S", 1, 0),
+    ("Z", 2, 0, "R"), ("Z", 2, 0, "L"), ("S", 1, 1), ("D", 0), ("C", 1), ("Z", 2, 1, "R"), ("Z", 2, 1, "L"),
+    ("Z", 3, 0, "L"), ("Z", 3, 0, "R"), ("S", 2, 0), ("E", 0), ("S", 2, 1), ("D", 1), ("Z", 3, 1, "R"),
+    ("Z", 3, 1, "L"), ("S", 3, 0), ("C", 2), ("S", 3, 1), ("F", 0), ("C", 3), ("D", 2), ("R", 0, 0, "R"),
+    ("R", 0, 0, "L"), ("E", 1), ("R", 0, 1, "R"), ("D", 3), ("R", 0, 1, "L"), ("E", 2), ("R", 0, 2, "R"), ("F", 1),
+    ("R", 0, 2, "L"), ("E", 3), ("F", 2), ("R", 1, 0, "R"), ("R", 1, 0, "L"), ("R", 2, 0, "R"), ("R", 1, 1, "R"),
+    ("R", 2, 0, "L"), ("R", 1, 1, "L"), ("F", 3), ("R", 2, 1, "R"), ("R", 2, 1, "L"), ("R", 1, 2, "R"),
+    ("R", 1, 2, "L"), ("R", 3, 0, "R"), ("R", 3, 0, "L"), ("R", 2, 2, "R"), ("R", 2, 2, "L"), ("R", 3, 1, "R"),
+    ("R", 3, 1, "L"), ("W", 2), ("R", 2, 3, "R"), ("R", 2, 3, "L"), ("R", 3, 2, "R"), ("R", 3, 2, "L"),
+    ("R", 1, 3, "L"), ("R", 1, 3, "R"), ("H", 2), ("R", 3, 3, "R"), ("R", 3, 3, "L"), ("R", 0, 3, "L"),
+    ("R", 0, 3, "R"), ("H", 1), ("W", 4), ("H", 3), ("W", 1), ("W", 0), ("H", 0), ("W", 3), ("FIN",),
 )
 
 
@@ -120,41 +115,42 @@
     fetch[0].wait()
     fetch[1].wait()
 
-    def do_a():
-        for j in (1, 2, 3):
-            send(TK.at[:, z], X.at[j, :, rows_of(0)], a_sem, j - 1, y_peer[j])
-
-    def do_j():
-        for r in range(8):
+    def fill(distances):
+        for r in distances:
             for a in range(2):
                 X[0, a, rows_of(PLACE[r])] = TK[a, (z + r) % 8]
+
+    def do_a():
+        fill((0, 4))
+        for j in (1, 2, 3):
+            send(X.at[0, :, rows_of(0, 2)], X.at[j, :, rows_of(0, 2)], a_sem, j - 1, y_peer[j])
+
+    def do_j():
+        fill((1, 2, 3, 5, 6, 7))
         send(X.at[0, :, 0:128], X.at[0, :, 128:256], j_sem, 0, sibling)
 
-    def z_piece(j, place, s, d):
-        rows = rows_of(place)
-        return X.at[j, :, rows] if s < 3 else X.at[j, "RL".index(d), rows]
-
-    def z_index(j, s, d):
-        return ((j - 1) * 4 + s) * 2 + "RL".index(d)
+    def z_rows(s, d):
+        return rows_of(2 if d == "R" else 4, 2) if s == 0 else rows_of(7 if d == "R" else 6)
 
     def z_arrived(j, s, d):
-        place = PLACE[7 - s if d == "R" else s + 1]
-        arrived(z_piece(j, place, s, d), z_sem, z_index(j, s, d))
+        arrived(X.at[j, :, z_rows(s, d)], z_sem, ((j - 1) * 2 + s) * 2 + "RL".index(d))
 
     def do_z(j, s, d):
         if s == 0:
-            arrived(X.at[j, :, rows_of(0)], a_sem, j - 1)
+            arrived(X.at[j, :, rows_of(0, 2)], a_sem, j - 1)
+            source = rows_of(0, 2)
         else:
-            z_arrived(j, s - 1, d)
-        place = PLACE[(8 - s) % 8 if d == "R" else s]
-        to = PLACE[7 - s if d == "R" else s + 1]
-        send(z_piece(j, place, s, d), z_piece(j, to, s, d), z_sem, z_index(j, s, d), ring[d])
+            z_arrived(j, 0, d)
+            source = rows_of(2 if d == "R" else 4)
+        index = ((j - 1) * 2 + s) * 2 + "RL".index(d)
+        send(X.at[j, :, source], X.at[j, :, z_rows(s, d)], z_sem, index, ring[d])
 
     def do_s(j, part):
-        for s in STEPS_OF[part]:
-            z_arrived(j, s, "R")
-            z_arrived(j, s, "L")
-        q, n = PLACES_OF[part]
+        if part == 0:
+            arrived(X.at[j, :, rows_of(0, 2)], a_sem, j - 1)
+        for d in "RL":
+            z_arrived(j, part, d)
+        q, n = ((0, 6), (6, 2))[part]
         send(X.at[j, :, rows_of(q, n)], X.at[j, :, rows_of(8 + q, n)], c_sem, j - 1, sibling)
 
     def do_c(j):
@@ -260,10 +256,10 @@
         stores.append(pltpu.make_async_copy(OB.at[1], grad_tokens, local_sem.at[7]))
         stores[2].start()
         stores[3].start()
-        all_left(FS, a_sem)
+        all_left(X.at[1:4, :, 0:32], a_sem)
         all_left(X.at[0, :, 0:128], j_sem)
         all_left(X.at[1:4, :, 0:128], c_sem)
-        all_left(X.at[1:4, :, 0:112], z_sem)
+        all_left(X.at[1:4, :, 0:96], z_sem)
         all_left(PR, p_sem)
         all_left(YS, y_sem)
         all_left(PR, h_sem)
@@ -341,7 +337,7 @@
             dma, dma((3,)),
             dma, dma((1,)),
             dma, dma((3,)),
-            dma, dma((24,)),
+            dma, dma((12,)),
             dma, dma((4,)),
             dma, dma((4,)),
             dma, dma((4,)),

time: 108 us -> 96.2 us (0.89)
  the two profiles are of different devices: /device:TPU:24 before, /device:TPU:2 now
where the time goes in v6:
time: 96.2 us; the launch traced here: 96 us
  Pallas kernels  95.4 us (99%)
    pallas_call x1, Pallas kernels, shards(): pl.pallas_call(kernel, out_shape=shapes, in_specs=[any_space] * 4, out_sp...  92.9 us
    pallas_call x1, Pallas kernels, shards(): pl.pallas_call(hand_out, out_shape=shapes, in_specs=[any_space] * 4, out_...  2.45 us

profile of v6, /device:TPU:2, one launch (start us, length us, event | category | flops | bytes accessed | tf_op | source)
XLA Modules:
  0.0 96.0 jit_solution(17628724538874694029)
XLA Ops:
  0.6 92.9 %shard_map.75 = (bf16[16,1152]{1,0:T(8,128)(2,1)}, bf16[16,1152]{1,0:T(8,128)(2,1)}, bf16[1152,384]{1,0:T(8,128)(2,1)}, bf16[384,1152]{1,0:T(8,128)(2,1)}) custom-call(bf16[8,16,1152]{2,1,0:T(8,128)(2,1)} %bitcast.2, bf16[1152,384]{1,0:T(8,128)(2,1)} %weight_in.1, bf16[384,1152]{1,0:T(8,128)(2,1)} %weight_out.1, bf16[8,16,1152]{2,1,0:T(8,128)(2,1)} %bitcast.3), custom_call_target="tpu_custom_call" | custom-call | flops 5436000256 | bytes 8000000 | tf_op jit(solution)/shard_map/pallas_call | solution.py:308
  93.6 2.4 %shard_map.76 = (bf16[16,1152]{1,0:T(8,128)(2,1)}, bf16[16,1152]{1,0:T(8,128)(2,1)}, bf16[1152,384]{1,0:T(8,128)(2,1)}, bf16[384,1152]{1,0:T(8,128)(2,1)}) custom-call(bf16[16,1152]{1,0:T(8,128)(2,1)} %get-tuple-element.8.refs_0_, bf16[16,1152]{1,0:T(8,128)(2,1)} %get-tuple-element.9.refs_1_, bf16[1152,384]{1,0:T(8,128)(2,1)} %get-tuple-element.10.refs_2_, ...), custom_call_target="tpu_custom_call" | custom-call | tf_op jit(solution)/shard_map/pallas_call | solution.py:353

commit v7 on v6

--- a/solution.py
+++ b/solution.py
@@ -11,18 +11,21 @@
 
 PLACE = {0: 0, 4: 1, 7: 2, 3: 3, 1: 4, 5: 5, 2: 6, 6: 7}
 ORDER = (
-    ("A",), ("J",), ("Z", 1, 0, "R"), ("Z", 1, 0, "L"), ("C", 0), ("Z", 1, 1, "R"), ("Z", 1, 1, "L"), ("S", 1, 0),
-    ("Z", 2, 0, "R"), ("Z", 2, 0, "L"), ("S", 1, 1), ("D", 0), ("C", 1), ("Z", 2, 1, "R"), ("Z", 2, 1, "L"),
-    ("Z", 3, 0, "L"), ("Z", 3, 0, "R"), ("S", 2, 0), ("E", 0), ("S", 2, 1), ("D", 1), ("Z", 3, 1, "R"),
-    ("Z", 3, 1, "L"), ("S", 3, 0), ("C", 2), ("S", 3, 1), ("F", 0), ("C", 3), ("D", 2), ("R", 0, 0, "R"),
-    ("R", 0, 0, "L"), ("E", 1), ("R", 0, 1, "R"), ("D", 3), ("R", 0, 1, "L"), ("E", 2), ("R", 0, 2, "R"), ("F", 1),
-    ("R", 0, 2, "L"), ("E", 3), ("F", 2), ("R", 1, 0, "R"), ("R", 1, 0, "L"), ("R", 2, 0, "R"), ("R", 1, 1, "R"),
-    ("R", 2, 0, "L"), ("R", 1, 1, "L"), ("F", 3), ("R", 2, 1, "R"), ("R", 2, 1, "L"), ("R", 1, 2, "R"),
-    ("R", 1, 2, "L"), ("R", 3, 0, "R"), ("R", 3, 0, "L"), ("R", 2, 2, "R"), ("R", 2, 2, "L"), ("R", 3, 1, "R"),
-    ("R", 3, 1, "L"), ("W", 2), ("R", 2, 3, "R"), ("R", 2, 3, "L"), ("R", 3, 2, "R"), ("R", 3, 2, "L"),
-    ("R", 1, 3, "L"), ("R", 1, 3, "R"), ("H", 2), ("R", 3, 3, "R"), ("R", 3, 3, "L"), ("R", 0, 3, "L"),
-    ("R", 0, 3, "R"), ("H", 1), ("W", 4), ("H", 3), ("W", 1), ("W", 0), ("H", 0), ("W", 3), ("FIN",),
+    ("A",), ("J",), ("Z", 1, 0, "L"), ("Z", 1, 0, "R"), ("C", 0), ("Z", 2, 0, "L"), ("Z", 2, 0, "R"),
+    ("Z", 1, 1, "L"), ("Z", 1, 1, "R"), ("S", 1, 0), ("Z", 2, 1, "L"), ("Z", 2, 1, "R"), ("Z", 3, 0, "L"),
+    ("Z", 3, 0, "R"), ("S", 1, 1), ("S", 2, 0), ("D", 0), ("C", 1), ("S", 2, 1), ("Z", 3, 1, "L"), ("S", 3, 0),
+    ("Z", 3, 1, "R"), ("C", 2), ("D", 1), ("E", 0), ("S", 3, 1), ("C", 3), ("D", 2), ("E", 1), ("F", 0), ("D", 3),
+    ("E", 2), ("R", 0, 0, "R"), ("R", 0, 0, "L"), ("F", 1), ("R", 0, 1, "R"), ("R", 0, 1, "L"), ("E", 3), ("F", 2),
+    ("R", 1, 0, "R"), ("R", 1, 0, "L"), ("R", 0, 2, "R"), ("R", 0, 2, "L"), ("R", 2, 0, "R"), ("R", 1, 1, "R"),
+    ("R", 2, 0, "L"), ("F", 3), ("R", 1, 1, "L"), ("R", 2, 1, "R"), ("R", 2, 1, "L"), ("R", 3, 0, "R"),
+    ("R", 3, 0, "L"), ("R", 1, 2, "R"), ("R", 1, 2, "L"), ("R", 2, 2, "R"), ("R", 2, 2, "L"), ("R", 3, 1, "R"),
+    ("R", 3, 1, "L"), ("W", 0), ("W", 3), ("R", 2, 3, "R"), ("R", 2, 3, "L"), ("R", 1, 3, "R"), ("R", 1, 3, "L"),
+    ("H", 3), ("R", 0, 3, "R"), ("H", 2), ("W", 1), ("H", 1), ("R", 0, 3, "L"), ("W", 2), ("W", 4), ("H", 0),
+    ("FIN",),
 )
+
+
+TWO_STEP = (3,)
 
 
 def gelu_both(pre_value, grad_value):
@@ -49,9 +52,9 @@
 def kernel(
     tokens, weight_in, weight_out, grad_out,
     layer_out, grad_tokens, grad_weight_in, grad_weight_out,
-    TK, X, WI, WO, PS, PR, YS, YR, HC, HT, GT, SS, SR, OP, ZS, ZR, FS, FR, FO, OB, GI, GO,
+    TK, X, WI, WO, PS, PR, YS, YR, HC, HT, GT, SS, SR, OP, ZS, ZR, FS, FR, GS, GR, FO, OB, GI, GO,
     local_sem, a_send, a_recv, j_send, j_recv, c_send, c_recv, z_send, z_recv,
-    p_send, p_recv, y_send, y_recv, h_send, h_recv, s_send, s_recv, r_send, r_recv, f_send, f_recv,
+    p_send, p_recv, y_send, y_recv, h_send, h_recv, s_send, s_recv, r_send, r_recv, q_send, f_send, f_recv, g_send, g_recv,
 ):
     dp = lax.axis_index("dp")
     row = lax.axis_index("row")
@@ -66,6 +69,8 @@
     ring = {"R": device(z=(z + 1) % 8), "L": device(z=(z + 7) % 8)}
     across = device(half=1 - half)
     y_peer = {1: device(y=y + 1 - 2 * (y % 2)), 2: device(y=(y + 2) % 4), 3: device(y=3 - y)}
+    far = device(z=(z + 4) % 8)
+    far_peer = {j: {**y_peer[j], "col": (z + 4) % 8} for j in (1, 2, 3)}
     x_at = {m: (x + m) % 4 for m in (1, 2, 3)}
     x_peer = {m: device(x=x_at[m]) for m in (1, 2, 3)}
 
@@ -95,11 +100,14 @@
 
     a_sem, j_sem, c_sem, z_sem = (a_send, a_recv), (j_send, j_recv), (c_send, c_recv), (z_send, z_recv)
     p_sem, y_sem, h_sem, s_sem = (p_send, p_recv), (y_send, y_recv), (h_send, h_recv), (s_send, s_recv)
-    r_sem, f_sem = (r_send, r_recv), (f_send, f_recv)
+    f_sem, g_sem = (f_send, f_recv), (g_send, g_recv)
+    ring_sem, two_sem = (r_send, r_recv), (q_send, r_recv)
+    r_sems = [two_sem if j in TWO_STEP else ring_sem for j in range(4)]
 
     barrier = pltpu.get_barrier_semaphore()
     peers = [sibling, *ring.values(), *y_peer.values(), *x_peer.values()]
     peers += [across]
+    peers += [far if j == 0 else far_peer[j] for j in TWO_STEP]
     for peer in peers:
         pl.semaphore_signal(barrier, inc=1, device_id=peer, device_id_type=MESH)
     fetch = [
@@ -194,40 +202,58 @@
     def r_index(j, i, d):
         return (j * 4 + i) * 2 + "RL".index(d)
 
-    def r_ref(buffer, j, i, d):
-        direction = "RL".index(d)
-        if i == 0:
-            return buffer.at[j, i, direction, direction]
-        return buffer.at[j, i, direction]
-
     def both_cores(j, r, a):
         rows = rows_of(PLACE[r])
         return OP[j, a, rows] + SR[j, a, rows].astype(F32)
 
-    def received(j, i, d, a):
-        return ZR[j, i, "RL".index(d), a].astype(F32)
+    def r_parts(j, i, d):
+        direction = "RL".index(d)
+        if j in TWO_STEP:
+            if i == 0:
+                return ((2 if d == "R" else 6, (0, 1), 0),)
+            return ((1, (0, 1), 1), (5, (0, 1), 2)) if d == "R" else ((7, (0, 1), 1), (3, (0, 1), 2))
+        return ((4 - i if d == "R" else 4 + i, (0, 1) if i else (direction,), i),)
+
+    def r_ref(buffer, j, i, d):
+        direction = "RL".index(d)
+        if j in TWO_STEP:
+            return buffer.at[j, 0, direction] if i == 0 else buffer.at[j, 1:3, direction]
+        return buffer.at[j, i, direction] if i else buffer.at[j, i, direction, direction]
+
+    def received(j, slot, d, a):
+        return ZR[j, slot, "RL".index(d), a].astype(F32)
 
     def do_r(j, i, d):
         direction = "RL".index(d)
-        for a in (0, 1) if i else (direction,):
+        for a in (0, 1) if i or j in TWO_STEP else (direction,):
             arrived(SR.at[j, a], s_sem, j * 2 + a)
-        r = 4 - i if d == "R" else 4 + i
         if i:
-            arrived(r_ref(ZR, j, i - 1, d), r_sem, r_index(j, i - 1, d))
-        for a in (0, 1) if i else (direction,):
-            total = both_cores(j, r, a)
-            if i > 1 or (i == 1 and a == direction):
-                total = total + received(j, i - 1, d, a)
-            ZS[j, i, direction, a] = total.astype(BF16)
-        send(r_ref(ZS, j, i, d), r_ref(ZR, j, i, d), r_sem, r_index(j, i, d), ring[d])
+            arrived(r_ref(ZR, j, i - 1, d), r_sems[j], r_index(j, i - 1, d))
+        for r, arrays, slot in r_parts(j, i, d):
+            for a in arrays:
+                total = both_cores(j, r, a)
+                if j in TWO_STEP:
+                    adds = i == 1 and slot == 1
+                else:
+                    adds = i > 1 or (i == 1 and a == direction)
+                if adds:
+                    total = total + received(j, i - 1, d, a)
+                ZS[j, slot, direction, a] = total.astype(BF16)
+        send(r_ref(ZS, j, i, d), r_ref(ZR, j, i, d), r_sems[j], r_index(j, i, d), ring[d])
 
     def do_h(j):
+        last = 1 if j in TWO_STEP else 3
         for a in (0, 1):
             arrived(SR.at[j, a], s_sem, j * 2 + a)
         for d in "RL":
-            arrived(r_ref(ZR, j, 3, d), r_sem, r_index(j, 3, d))
+            arrived(r_ref(ZR, j, last, d), r_sems[j], r_index(j, last, d))
+        if j in TWO_STEP:
+            for a in (0, 1):
+                total = both_cores(j, 4, a) + received(j, 2, "R", a) + received(j, 2, "L", a)
+                GS[j, a] = total.astype(BF16)
+            send(GS.at[j], GR.at[j], g_sem, j, far_peer[j] if j else far)
         for a in (0, 1):
-            total = both_cores(j, 0, a) + received(j, 3, "R", a) + received(j, 3, "L", a)
+            total = both_cores(j, 0, a) + received(j, last, "R", a) + received(j, last, "L", a)
             if j == 0:
                 FO[a] = total
             else:
@@ -251,6 +277,9 @@
         for j in (1, 2, 3):
             arrived(FR.at[j - 1], f_sem, j - 1)
             total = total + FR[j - 1].astype(F32)
+        for j in TWO_STEP:
+            arrived(GR.at[j], g_sem, j)
+            total = total + GR[j].astype(F32)
         OB[...] = total.astype(BF16)
         stores.append(pltpu.make_async_copy(OB.at[0], layer_out, local_sem.at[6]))
         stores.append(pltpu.make_async_copy(OB.at[1], grad_tokens, local_sem.at[7]))
@@ -264,7 +293,10 @@
         all_left(YS, y_sem)
         all_left(PR, h_sem)
         all_left(SS, s_sem)
-        all_left(X.at[:, :, 0:112], r_sem)
+        ring_batches = [j for j in range(4) if j not in TWO_STEP]
+        all_left(X.at[0:len(ring_batches), :, 0:112], ring_sem)
+        all_left(X.at[0:len(TWO_STEP), :, 0:96], two_sem)
+        all_left(GS.at[0:len(TWO_STEP)], g_sem)
         all_left(FS, f_sem)
         for copy in stores:
             copy.wait()
@@ -329,6 +361,8 @@
             pltpu.VMEM((4, 4, 2, 2, 16, 1152), BF16),
             pltpu.VMEM((3, 2, 16, 1152), BF16),
             pltpu.VMEM((3, 2, 16, 1152), BF16),
+            pltpu.VMEM((4, 2, 16, 1152), BF16),
+            pltpu.VMEM((4, 2, 16, 1152), BF16),
             pltpu.VMEM((2, 16, 1152), F32),
             pltpu.VMEM((2, 16, 1152), BF16),
             pltpu.VMEM((1152, 384), BF16),
@@ -342,8 +376,9 @@
             dma, dma((4,)),
             dma, dma((4,)),
             dma, dma((8,)),
-            dma, dma((32,)),
+            dma, dma((32,)), dma,
             dma, dma((3,)),
+            dma, dma((4,)),
         ],
         compiler_params=pltpu.CompilerParams(
             collective_id=0, has_side_effects=True, vmem_limit_bytes=56 * 1024 * 1024

time: 96.2 us -> 97 us (level)
  the two profiles are of different devices: /device:TPU:2 before, /device:TPU:8 now
where the time goes in v7:
time: 97 us; the launch traced here: 96.9 us
  Pallas kernels  96.2 us (99%)
    pallas_call x1, Pallas kernels, shards(): pl.pallas_call(kernel, out_shape=shapes, in_specs=[any_space] * 4, out_sp...  93.8 us
    pallas_call x1, Pallas kernels, shards(): pl.pallas_call(hand_out, out_shape=shapes, in_specs=[any_space] * 4, out_...  2.45 us

profile of v7, /device:TPU:8, one launch (start us, length us, event | category | flops | bytes accessed | tf_op | source)
XLA Modules:
  0.0 96.9 jit_solution(18439132311301431563)
XLA Ops:
  0.6 93.8 %shard_map.75 = (bf16[16,1152]{1,0:T(8,128)(2,1)}, bf16[16,1152]{1,0:T(8,128)(2,1)}, bf16[1152,384]{1,0:T(8,128)(2,1)}, bf16[384,1152]{1,0:T(8,128)(2,1)}) custom-call(bf16[8,16,1152]{2,1,0:T(8,128)(2,1)} %bitcast.2, bf16[1152,384]{1,0:T(8,128)(2,1)} %weight_in.1, bf16[384,1152]{1,0:T(8,128)(2,1)} %weight_out.1, bf16[8,16,1152]{2,1,0:T(8,128)(2,1)} %bitcast.3), custom_call_target="tpu_custom_call" | custom-call | flops 5436000256 | bytes 8000000 | tf_op jit(solution)/shard_map/pallas_call | solution.py:340
  94.4 2.4 %shard_map.76 = (bf16[16,1152]{1,0:T(8,128)(2,1)}, bf16[16,1152]{1,0:T(8,128)(2,1)}, bf16[1152,384]{1,0:T(8,128)(2,1)}, bf16[384,1152]{1,0:T(8,128)(2,1)}) custom-call(bf16[16,1152]{1,0:T(8,128)(2,1)} %get-tuple-element.8.refs_0_, bf16[16,1152]{1,0:T(8,128)(2,1)} %get-tuple-element.9.refs_1_, bf16[1152,384]{1,0:T(8,128)(2,1)} %get-tuple-element.10.refs_2_, ...), custom_call_target="tpu_custom_call" | custom-call | tf_op jit(solution)/shard_map/pallas_call | solution.py:388

commit v8 on v7

--- a/solution.py
+++ b/solution.py
@@ -11,21 +11,24 @@
 
 PLACE = {0: 0, 4: 1, 7: 2, 3: 3, 1: 4, 5: 5, 2: 6, 6: 7}
 ORDER = (
-    ("A",), ("J",), ("Z", 1, 0, "L"), ("Z", 1, 0, "R"), ("C", 0), ("Z", 2, 0, "L"), ("Z", 2, 0, "R"),
-    ("Z", 1, 1, "L"), ("Z", 1, 1, "R"), ("S", 1, 0), ("Z", 2, 1, "L"), ("Z", 2, 1, "R"), ("Z", 3, 0, "L"),
-    ("Z", 3, 0, "R"), ("S", 1, 1), ("S", 2, 0), ("D", 0), ("C", 1), ("S", 2, 1), ("Z", 3, 1, "L"), ("S", 3, 0),
-    ("Z", 3, 1, "R"), ("C", 2), ("D", 1), ("E", 0), ("S", 3, 1), ("C", 3), ("D", 2), ("E", 1), ("F", 0), ("D", 3),
-    ("E", 2), ("R", 0, 0, "R"), ("R", 0, 0, "L"), ("F", 1), ("R", 0, 1, "R"), ("R", 0, 1, "L"), ("E", 3), ("F", 2),
-    ("R", 1, 0, "R"), ("R", 1, 0, "L"), ("R", 0, 2, "R"), ("R", 0, 2, "L"), ("R", 2, 0, "R"), ("R", 1, 1, "R"),
-    ("R", 2, 0, "L"), ("F", 3), ("R", 1, 1, "L"), ("R", 2, 1, "R"), ("R", 2, 1, "L"), ("R", 3, 0, "R"),
-    ("R", 3, 0, "L"), ("R", 1, 2, "R"), ("R", 1, 2, "L"), ("R", 2, 2, "R"), ("R", 2, 2, "L"), ("R", 3, 1, "R"),
-    ("R", 3, 1, "L"), ("W", 0), ("W", 3), ("R", 2, 3, "R"), ("R", 2, 3, "L"), ("R", 1, 3, "R"), ("R", 1, 3, "L"),
-    ("H", 3), ("R", 0, 3, "R"), ("H", 2), ("W", 1), ("H", 1), ("R", 0, 3, "L"), ("W", 2), ("W", 4), ("H", 0),
-    ("FIN",),
+    ("A",), ("J",), ("Z", 1, 0, "R"), ("Z", 1, 0, "L"), ("C", 0, 0), ("Z", 2, 0, "R"), ("Z", 2, 0, "L"),
+    ("C", 0, 1), ("Z", 1, 1, "R"), ("Z", 1, 1, "L"), ("S", 1, 0), ("Z", 2, 1, "R"), ("Z", 2, 1, "L"),
+    ("Z", 3, 0, "R"), ("Z", 3, 0, "L"), ("S", 1, 1), ("D", 0), ("S", 2, 0), ("S", 2, 1), ("C", 1, 0), ("C", 1, 1),
+    ("Z", 3, 1, "R"), ("Z", 3, 1, "L"), ("S", 3, 0), ("C", 2, 0), ("C", 2, 1), ("S", 3, 1), ("D", 1), ("C", 3, 0),
+    ("C", 3, 1), ("D", 2), ("E", 1), ("D", 3), ("E", 2), ("F", 1, 0), ("F", 1, 1), ("E", 3), ("E", 0), ("F", 2, 0),
+    ("F", 2, 1), ("K",), ("T", 1), ("T", 2), ("R", 2, 0, "R"), ("F", 3, 0), ("R", 2, 0, "L"), ("F", 3, 1),
+    ("T", 3), ("R", 2, 1, "R"), ("R", 2, 1, "L"), ("R", 3, 0, "R"), ("F", 0, 0), ("R", 3, 0, "L"), ("F", 0, 1),
+    ("R", 2, 2, "R"), ("R", 2, 2, "L"), ("R", 3, 1, "R"), ("T", 0), ("R", 3, 1, "L"), ("R", 0, 0, "R"),
+    ("W", 0, 1), ("R", 0, 0, "L"), ("R", 2, 3, "R"), ("R", 2, 3, "L"), ("W", 4, 1), ("R", 3, 2, "R"),
+    ("R", 3, 2, "L"), ("R", 0, 1, "R"), ("R", 0, 1, "L"), ("W", 1, 1), ("W", 2, 0), ("H", 2), ("R", 3, 3, "R"),
+    ("R", 3, 3, "L"), ("R", 0, 2, "R"), ("R", 0, 2, "L"), ("W", 3, 0), ("W", 1, 0), ("H", 3), ("W", 4, 0),
+    ("R", 0, 3, "R"), ("R", 0, 3, "L"), ("W", 3, 1), ("W", 2, 1), ("W", 0, 0), ("H", 0), ("FIN",),
 )
 
 
-TWO_STEP = (3,)
+TWO_STEP = ()
+RETURNED = (2, 3)
+FOLD_INTO = 0
 
 
 def gelu_both(pre_value, grad_value):
@@ -52,9 +55,9 @@
 def kernel(
     tokens, weight_in, weight_out, grad_out,
     layer_out, grad_tokens, grad_weight_in, grad_weight_out,
-    TK, X, WI, WO, PS, PR, YS, YR, HC, HT, GT, SS, SR, OP, ZS, ZR, FS, FR, GS, GR, FO, OB, GI, GO,
+    TK, X, WI, WO, PS, PR, YS, YR, HC, HT, GT, SS, SR, OP, ZS, ZR, FS, FR, GS, GR, KS, KR, FO, OB, GI, GO,
     local_sem, a_send, a_recv, j_send, j_recv, c_send, c_recv, z_send, z_recv,
-    p_send, p_recv, y_send, y_recv, h_send, h_recv, s_send, s_recv, r_send, r_recv, q_send, f_send, f_recv, g_send, g_recv,
+    p_send, p_recv, y_send, y_recv, h_send, h_recv, s_send, s_recv, r_send, r_recv, q_send, f_send, f_recv, g_send, g_recv, k_send, k_recv,
 ):
     dp = lax.axis_index("dp")
     row = lax.axis_index("row")
@@ -100,7 +103,7 @@
 
     a_sem, j_sem, c_sem, z_sem = (a_send, a_recv), (j_send, j_recv), (c_send, c_recv), (z_send, z_recv)
     p_sem, y_sem, h_sem, s_sem = (p_send, p_recv), (y_send, y_recv), (h_send, h_recv), (s_send, s_recv)
-    f_sem, g_sem = (f_send, f_recv), (g_send, g_recv)
+    f_sem, g_sem, k_sem = (f_send, f_recv), (g_send, g_recv), (k_send, k_recv)
     ring_sem, two_sem = (r_send, r_recv), (q_send, r_recv)
     r_sems = [two_sem if j in TWO_STEP else ring_sem for j in range(4)]
 
@@ -161,15 +164,16 @@
         q, n = ((0, 6), (6, 2))[part]
         send(X.at[j, :, rows_of(q, n)], X.at[j, :, rows_of(8 + q, n)], c_sem, j - 1, sibling)
 
-    def do_c(j):
+    def do_c(j, a):
         if j == 0:
             arrived(X.at[0, :, 128:256], j_sem, 0)
         else:
             arrived(X.at[j, :, 128:256], c_sem, j - 1)
-        PS[:, j, 0] = times(X[j, 0], WI[...]).astype(BF16).reshape(4, 64, 384)
-        PS[:, j, 1] = times_transposed(X[j, 1], WO[...]).astype(BF16).reshape(4, 64, 384)
-        for m in (2, 1, 3):
-            send(PS.at[x_at[m], j], PR.at[m - 1, j], p_sem, j, x_peer[m])
+        val = times(X[j, 0], WI[...]) if a == 0 else times_transposed(X[j, 1], WO[...])
+        PS[:, j, a] = val.astype(BF16).reshape(4, 64, 384)
+        if a == 1:
+            for m in (2, 1, 3):
+                send(PS.at[x_at[m], j], PR.at[m - 1, j], p_sem, j, x_peer[m])
 
     def do_d(j):
         arrived(PR.at[:, j], p_sem, j)
@@ -188,23 +192,39 @@
         for m in (2, 1, 3):
             send(HC.at[j, :, x], HC.at[j, :, x], h_sem, j, x_peer[m])
 
-    def do_f(j):
+    def do_f(j, a):
         arrived(PR.at[:, j], h_sem, j)
-        for a in (0, 1):
-            lhs = HC[j, a].reshape(256, 384)
-            val = times(lhs, WO[...]) if a == 0 else times_transposed(lhs, WI[...])
-            OP[j, a] = val[0:128]
-            SS[j, a] = val[128:256].astype(BF16)
-            send(SS.at[j, a], SR.at[j, a], s_sem, j * 2 + a, sibling)
+        lhs = HC[j, a].reshape(256, 384)
+        val = times(lhs, WO[...]) if a == 0 else times_transposed(lhs, WI[...])
+        OP[j, a] = val[0:128]
+        SS[j, a] = val[128:256].astype(BF16)
+        send(SS.at[j, a], SR.at[j, a], s_sem, j * 2 + a, sibling)
+
+    def do_t(j):
         HT[:, j * 256:(j + 1) * 256] = HC[j, 0].reshape(256, 384).T
         GT[:, j * 256:(j + 1) * 256] = HC[j, 1].reshape(256, 384).T
 
     def r_index(j, i, d):
         return (j * 4 + i) * 2 + "RL".index(d)
 
+    def here(j, arrays):
+        for a in arrays:
+            arrived(SR.at[j, a], s_sem, j * 2 + a)
+            if j == FOLD_INTO:
+                arrived(KR.at[a], k_sem, a)
+
     def both_cores(j, r, a):
         rows = rows_of(PLACE[r])
-        return OP[j, a, rows] + SR[j, a, rows].astype(F32)
+        total = OP[j, a, rows] + SR[j, a, rows].astype(F32)
+        if j == FOLD_INTO:
+            total = total + KR[a, rows].astype(F32)
+        return total
+
+    def do_k():
+        here(1, (0, 1))
+        for a in (0, 1):
+            KS[a] = (OP[1, a] + SR[1, a].astype(F32)).astype(BF16)
+            send(KS.at[a], KR.at[a], k_sem, a, y_peer[1])
 
     def r_parts(j, i, d):
         direction = "RL".index(d)
@@ -225,8 +245,7 @@
 
     def do_r(j, i, d):
         direction = "RL".index(d)
-        for a in (0, 1) if i or j in TWO_STEP else (direction,):
-            arrived(SR.at[j, a], s_sem, j * 2 + a)
+        here(j, (0, 1) if i or j in TWO_STEP else (direction,))
         if i:
             arrived(r_ref(ZR, j, i - 1, d), r_sems[j], r_index(j, i - 1, d))
         for r, arrays, slot in r_parts(j, i, d):
@@ -243,8 +262,7 @@
 
     def do_h(j):
         last = 1 if j in TWO_STEP else 3
-        for a in (0, 1):
-            arrived(SR.at[j, a], s_sem, j * 2 + a)
+        here(j, (0, 1))
         for d in "RL":
             arrived(r_ref(ZR, j, last, d), r_sems[j], r_index(j, last, d))
         if j in TWO_STEP:
@@ -261,10 +279,13 @@
         if j:
             send(FS.at[j - 1], FR.at[j - 1], f_sem, j - 1, y_peer[j])
 
-    def do_w(k):
+    def do_w(k, which):
         cols = pl.ds(k * 256, min(256, 1152 - k * 256))
-        GI[cols, :] = times(GT[...], X[:, 0, :, cols].reshape(1024, cols.size)).T.astype(BF16)
-        GO[:, cols] = times(HT[...], X[:, 1, :, cols].reshape(1024, cols.size)).astype(BF16)
+        rhs = X[:, which, :, cols].reshape(1024, cols.size)
+        if which == 0:
+            GI[cols, :] = times(GT[...], rhs).T.astype(BF16)
+        else:
+            GO[:, cols] = times(HT[...], rhs).astype(BF16)
 
     def do_fin():
         stores = [
@@ -274,7 +295,7 @@
         for copy in stores:
             copy.start()
         total = FO[...]
-        for j in (1, 2, 3):
+        for j in RETURNED:
             arrived(FR.at[j - 1], f_sem, j - 1)
             total = total + FR[j - 1].astype(F32)
         for j in TWO_STEP:
@@ -293,17 +314,19 @@
         all_left(YS, y_sem)
         all_left(PR, h_sem)
         all_left(SS, s_sem)
-        ring_batches = [j for j in range(4) if j not in TWO_STEP]
+        ring_batches = [j for j in (0, *RETURNED) if j not in TWO_STEP]
         all_left(X.at[0:len(ring_batches), :, 0:112], ring_sem)
-        all_left(X.at[0:len(TWO_STEP), :, 0:96], two_sem)
-        all_left(GS.at[0:len(TWO_STEP)], g_sem)
-        all_left(FS, f_sem)
+        if TWO_STEP:
+            all_left(X.at[0:len(TWO_STEP), :, 0:96], two_sem)
+            all_left(GS.at[0:len(TWO_STEP)], g_sem)
+        all_left(FS.at[0:len(RETURNED)], f_sem)
+        all_left(KS, k_sem)
         for copy in stores:
             copy.wait()
 
     steps = {
         "A": do_a, "J": do_j, "Z": do_z, "S": do_s, "C": do_c, "D": do_d, "E": do_e, "F": do_f,
-        "R": do_r, "H": do_h, "W": do_w, "FIN": do_fin,
+        "R": do_r, "H": do_h, "W": do_w, "T": do_t, "K": do_k, "FIN": do_fin,
     }
     weights_here = False
     for step in ORDER:
@@ -363,6 +386,8 @@
             pltpu.VMEM((3, 2, 16, 1152), BF16),
             pltpu.VMEM((4, 2, 16, 1152), BF16),
             pltpu.VMEM((4, 2, 16, 1152), BF16),
+            pltpu.VMEM((2, 128, 1152), BF16),
+            pltpu.VMEM((2, 128, 1152), BF16),
             pltpu.VMEM((2, 16, 1152), F32),
             pltpu.VMEM((2, 16, 1152), BF16),
             pltpu.VMEM((1152, 384), BF16),
@@ -379,6 +404,7 @@
             dma, dma((32,)), dma,
             dma, dma((3,)),
             dma, dma((4,)),
+            dma, dma((2,)),
         ],
         compiler_params=pltpu.CompilerParams(
             collective_id=0, has_side_effects=True, vmem_limit_bytes=56 * 1024 * 1024

time: 97 us -> 97.9 us (level)
  the two profiles are of different devices: /device:TPU:8 before, /device:TPU:4 now
where the time goes in v8:
time: 97.9 us; the launch traced here: 97.8 us
  Pallas kernels  97.2 us (99%)
    pallas_call x1, Pallas kernels, shards(): pl.pallas_call(kernel, out_shape=shapes, in_specs=[any_space] * 4, out_sp...  94.7 us
    pallas_call x1, Pallas kernels, shards(): pl.pallas_call(hand_out, out_shape=shapes, in_specs=[any_space] * 4, out_...  2.45 us

profile of v8, /device:TPU:4, one launch (start us, length us, event | category | flops | bytes accessed | tf_op | source)
XLA Modules:
  0.0 97.8 jit_solution(2998053839127600168)
XLA Ops:
  0.6 94.7 %shard_map.75 = (bf16[16,1152]{1,0:T(8,128)(2,1)}, bf16[16,1152]{1,0:T(8,128)(2,1)}, bf16[1152,384]{1,0:T(8,128)(2,1)}, bf16[384,1152]{1,0:T(8,128)(2,1)}) custom-call(bf16[8,16,1152]{2,1,0:T(8,128)(2,1)} %bitcast.2, bf16[1152,384]{1,0:T(8,128)(2,1)} %weight_in.1, bf16[384,1152]{1,0:T(8,128)(2,1)} %weight_out.1, bf16[8,16,1152]{2,1,0:T(8,128)(2,1)} %bitcast.3), custom_call_target="tpu_custom_call" | custom-call | flops 5436000256 | bytes 8000000 | tf_op jit(solution)/shard_map/pallas_call | solution.py:363
  95.4 2.4 %shard_map.76 = (bf16[16,1152]{1,0:T(8,128)(2,1)}, bf16[16,1152]{1,0:T(8,128)(2,1)}, bf16[1152,384]{1,0:T(8,128)(2,1)}, bf16[384,1152]{1,0:T(8,128)(2,1)}) custom-call(bf16[16,1152]{1,0:T(8,128)(2,1)} %get-tuple-element.8.refs_0_, bf16[16,1152]{1,0:T(8,128)(2,1)} %get-tuple-element.9.refs_1_, bf16[1152,384]{1,0:T(8,128)(2,1)} %get-tuple-element.10.refs_2_, ...), custom_call_target="tpu_custom_call" | custom-call | tf_op jit(solution)/shard_map/pallas_call | solution.py:414

commit v9 on v8

--- a/solution.py
+++ b/solution.py
@@ -11,24 +11,24 @@
 
 PLACE = {0: 0, 4: 1, 7: 2, 3: 3, 1: 4, 5: 5, 2: 6, 6: 7}
 ORDER = (
-    ("A",), ("J",), ("Z", 1, 0, "R"), ("Z", 1, 0, "L"), ("C", 0, 0), ("Z", 2, 0, "R"), ("Z", 2, 0, "L"),
-    ("C", 0, 1), ("Z", 1, 1, "R"), ("Z", 1, 1, "L"), ("S", 1, 0), ("Z", 2, 1, "R"), ("Z", 2, 1, "L"),
-    ("Z", 3, 0, "R"), ("Z", 3, 0, "L"), ("S", 1, 1), ("D", 0), ("S", 2, 0), ("S", 2, 1), ("C", 1, 0), ("C", 1, 1),
-    ("Z", 3, 1, "R"), ("Z", 3, 1, "L"), ("S", 3, 0), ("C", 2, 0), ("C", 2, 1), ("S", 3, 1), ("D", 1), ("C", 3, 0),
-    ("C", 3, 1), ("D", 2), ("E", 1), ("D", 3), ("E", 2), ("F", 1, 0), ("F", 1, 1), ("E", 3), ("E", 0), ("F", 2, 0),
-    ("F", 2, 1), ("K",), ("T", 1), ("T", 2), ("R", 2, 0, "R"), ("F", 3, 0), ("R", 2, 0, "L"), ("F", 3, 1),
-    ("T", 3), ("R", 2, 1, "R"), ("R", 2, 1, "L"), ("R", 3, 0, "R"), ("F", 0, 0), ("R", 3, 0, "L"), ("F", 0, 1),
-    ("R", 2, 2, "R"), ("R", 2, 2, "L"), ("R", 3, 1, "R"), ("T", 0), ("R", 3, 1, "L"), ("R", 0, 0, "R"),
-    ("W", 0, 1), ("R", 0, 0, "L"), ("R", 2, 3, "R"), ("R", 2, 3, "L"), ("W", 4, 1), ("R", 3, 2, "R"),
-    ("R", 3, 2, "L"), ("R", 0, 1, "R"), ("R", 0, 1, "L"), ("W", 1, 1), ("W", 2, 0), ("H", 2), ("R", 3, 3, "R"),
-    ("R", 3, 3, "L"), ("R", 0, 2, "R"), ("R", 0, 2, "L"), ("W", 3, 0), ("W", 1, 0), ("H", 3), ("W", 4, 0),
-    ("R", 0, 3, "R"), ("R", 0, 3, "L"), ("W", 3, 1), ("W", 2, 1), ("W", 0, 0), ("H", 0), ("FIN",),
+    ("A",), ("J",), ("C", 0, 0), ("C", 0, 1), ("Z", 1, 0, "L"), ("Z", 1, 0, "R"), ("Z", 2, 0, "R"),
+    ("Z", 2, 0, "L"), ("Z", 1, 1, "R"), ("Z", 1, 1, "L"), ("D", 0), ("S", 1, 0), ("Z", 2, 1, "R"),
+    ("Z", 2, 1, "L"), ("S", 1, 1), ("Z", 3, 0, "L"), ("Z", 3, 0, "R"), ("S", 2, 0), ("C", 1, 0), ("S", 2, 1),
+    ("C", 1, 1), ("Z", 3, 1, "L"), ("Z", 3, 1, "R"), ("C", 2, 0), ("C", 2, 1), ("S", 3, 0), ("D", 1), ("S", 3, 1),
+    ("E", 0), ("C", 3, 0), ("C", 3, 1), ("D", 2), ("F", 0, 0), ("E", 1), ("D", 3), ("F", 0, 1), ("R", 0, 0, "R"),
+    ("E", 2), ("R", 0, 0, "L"), ("F", 1, 0), ("T", 0), ("F", 1, 1), ("R", 0, 1, "R"), ("R", 0, 1, "L"), ("E", 3),
+    ("R", 1, 0, "R"), ("R", 1, 0, "L"), ("F", 2, 0), ("R", 0, 2, "R"), ("R", 0, 2, "L"), ("F", 2, 1),
+    ("R", 1, 1, "R"), ("R", 1, 1, "L"), ("F", 3, 0), ("F", 3, 1), ("R", 2, 0, "R"), ("R", 2, 0, "L"), ("T", 3),
+    ("R", 1, 2, "R"), ("R", 1, 2, "L"), ("R", 3, 0, "L"), ("R", 3, 0, "R"), ("R", 2, 1, "R"), ("R", 2, 1, "L"),
+    ("T", 1), ("R", 1, 3, "R"), ("T", 2), ("W", 2, 0), ("R", 3, 1, "L"), ("R", 3, 1, "R"), ("R", 1, 3, "L"),
+    ("W", 4, 0), ("W", 3, 0), ("H", 2), ("H", 3), ("W", 4, 1), ("H", 1), ("R", 0, 3, "R"), ("R", 0, 3, "L"),
+    ("W", 3, 1), ("W", 0, 0), ("W", 2, 1), ("W", 0, 1), ("W", 1, 0), ("W", 1, 1), ("H", 0), ("FIN",),
 )
 
 
-TWO_STEP = ()
-RETURNED = (2, 3)
-FOLD_INTO = 0
+TWO_STEP = (2,3,)
+RETURNED = (1, 2, 3)
+FOLD_INTO = None
 
 
 def gelu_both(pre_value, grad_value):
@@ -320,7 +320,6 @@
             all_left(X.at[0:len(TWO_STEP), :, 0:96], two_sem)
             all_left(GS.at[0:len(TWO_STEP)], g_sem)
         all_left(FS.at[0:len(RETURNED)], f_sem)
-        all_left(KS, k_sem)
         for copy in stores:
             copy.wait()
 

time: 97.9 us -> 99.9 us (1.020)
  the two profiles are of different devices: /device:TPU:4 before, /device:TPU:8 now
where the time goes in v9:
time: 99.9 us; the launch traced here: 99.7 us
  Pallas kernels  99.1 us (99%)
    pallas_call x1, Pallas kernels, shards(): pl.pallas_call(kernel, out_shape=shapes, in_specs=[any_space] * 4, out_sp...  96.6 us
    pallas_call x1, Pallas kernels, shards(): pl.pallas_call(hand_out, out_shape=shapes, in_specs=[any_space] * 4, out_...  2.45 us

profile of v9, /device:TPU:8, one launch (start us, length us, event | category | flops | bytes accessed | tf_op | source)
XLA Modules:
  0.0 99.7 jit_solution(17889271369621733624)
XLA Ops:
  0.6 96.6 %shard_map.75 = (bf16[16,1152]{1,0:T(8,128)(2,1)}, bf16[16,1152]{1,0:T(8,128)(2,1)}, bf16[1152,384]{1,0:T(8,128)(2,1)}, bf16[384,1152]{1,0:T(8,128)(2,1)}) custom-call(bf16[8,16,1152]{2,1,0:T(8,128)(2,1)} %bitcast.2, bf16[1152,384]{1,0:T(8,128)(2,1)} %weight_in.1, bf16[384,1152]{1,0:T(8,128)(2,1)} %weight_out.1, bf16[8,16,1152]{2,1,0:T(8,128)(2,1)} %bitcast.3), custom_call_target="tpu_custom_call" | custom-call | flops 5436000256 | bytes 8000000 | tf_op jit(solution)/shard_map/pallas_call | solution.py:362
  97.3 2.4 %shard_map.76 = (bf16[16,1152]{1,0:T(8,128)(2,1)}, bf16[16,1152]{1,0:T(8,128)(2,1)}, bf16[1152,384]{1,0:T(8,128)(2,1)}, bf16[384,1152]{1,0:T(8,128)(2,1)}) custom-call(bf16[16,1152]{1,0:T(8,128)(2,1)} %get-tuple-element.8.refs_0_, bf16[16,1152]{1,0:T(8,128)(2,1)} %get-tuple-element.9.refs_1_, bf16[1152,384]{1,0:T(8,128)(2,1)} %get-tuple-element.10.refs_2_, ...), custom_call_target="tpu_custom_call" | custom-call | tf_op jit(solution)/shard_map/pallas_call | solution.py:413

commit v10 on v6

--- a/solution.py
+++ b/solution.py
@@ -19,9 +19,9 @@
     ("R", 0, 2, "L"), ("E", 3), ("F", 2), ("R", 1, 0, "R"), ("R", 1, 0, "L"), ("R", 2, 0, "R"), ("R", 1, 1, "R"),
     ("R", 2, 0, "L"), ("R", 1, 1, "L"), ("F", 3), ("R", 2, 1, "R"), ("R", 2, 1, "L"), ("R", 1, 2, "R"),
     ("R", 1, 2, "L"), ("R", 3, 0, "R"), ("R", 3, 0, "L"), ("R", 2, 2, "R"), ("R", 2, 2, "L"), ("R", 3, 1, "R"),
-    ("R", 3, 1, "L"), ("W", 2), ("R", 2, 3, "R"), ("R", 2, 3, "L"), ("R", 3, 2, "R"), ("R", 3, 2, "L"),
-    ("R", 1, 3, "L"), ("R", 1, 3, "R"), ("H", 2), ("R", 3, 3, "R"), ("R", 3, 3, "L"), ("R", 0, 3, "L"),
-    ("R", 0, 3, "R"), ("H", 1), ("W", 4), ("H", 3), ("W", 1), ("W", 0), ("H", 0), ("W", 3), ("FIN",),
+    ("R", 3, 1, "L"), ("W", 3), ("R", 2, 3, "R"), ("R", 2, 3, "L"), ("R", 3, 2, "R"), ("R", 3, 2, "L"), ("W", 4),
+    ("R", 1, 3, "L"), ("R", 1, 3, "R"), ("H", 2), ("R", 3, 3, "R"), ("R", 3, 3, "L"), ("W", 2), ("R", 0, 3, "L"),
+    ("R", 0, 3, "R"), ("H", 1), ("H", 3), ("W", 1), ("W", 0), ("H", 0), ("FIN",),
 )
 
 
@@ -284,16 +284,17 @@
 
 def hand_out(*refs):
     results, outputs, held, arrive, leave = refs[0:4], refs[4:8], refs[8:12], refs[12], refs[13]
-    order = (2, 3, 0, 1)
-    fetches = {i: pltpu.make_async_copy(results[i], held[i], arrive.at[i]) for i in order}
-    stores = {i: pltpu.make_async_copy(held[i], outputs[i], leave.at[i]) for i in order}
-    for i in order:
-        fetches[i].start()
-    for i in order:
-        fetches[i].wait()
-        stores[i].start()
-    for i in order:
-        stores[i].wait()
+    parts = [(i, pl.ds(half * rows, rows)) for half in (0, 1) for i, rows in ((2, 576), (3, 192))]
+    parts += [(i, pl.ds(0, 16)) for i in (0, 1)]
+    fetches = [pltpu.make_async_copy(results[i].at[p], held[i].at[p], arrive.at[n]) for n, (i, p) in enumerate(parts)]
+    stores = [pltpu.make_async_copy(held[i].at[p], outputs[i].at[p], leave.at[n]) for n, (i, p) in enumerate(parts)]
+    for fetch in fetches:
+        fetch.start()
+    for fetch, store in zip(fetches, stores):
+        fetch.wait()
+        store.start()
+    for store in stores:
+        store.wait()
 
 
 def shards(tokens, weight_in, weight_out, grad_out):
@@ -355,7 +356,7 @@
         out_shape=shapes,
         in_specs=[any_space] * 4,
         out_specs=(any_space,) * 4,
-        scratch_shapes=[*(pltpu.VMEM(shape.shape, BF16) for shape in shapes), dma((4,)), dma((4,))],
+        scratch_shapes=[*(pltpu.VMEM(shape.shape, BF16) for shape in shapes), dma((6,)), dma((6,))],
     )(*results)
 
 

time: 96.2 us -> 96.1 us (level)
  no operation moved by 1% of the time
where the time goes in v10:
time: 96.1 us; the launch traced here: 95.9 us
  Pallas kernels  95.3 us (99%)
    pallas_call x1, Pallas kernels, shards(): pl.pallas_call(kernel, out_shape=shapes, in_specs=[any_space] * 4, out_sp...  92.9 us
    pallas_call x1, Pallas kernels, shards(): pl.pallas_call(hand_out, out_shape=shapes, in_specs=[any_space] * 4, out_...  2.33 us

profile of v10, /device:TPU:2, one launch (start us, length us, event | category | flops | bytes accessed | tf_op | source)
XLA Modules:
  0.0 95.9 jit_solution(15586478276516089086)
XLA Ops:
  0.6 92.9 %shard_map.75 = (bf16[16,1152]{1,0:T(8,128)(2,1)}, bf16[16,1152]{1,0:T(8,128)(2,1)}, bf16[1152,384]{1,0:T(8,128)(2,1)}, bf16[384,1152]{1,0:T(8,128)(2,1)}) custom-call(bf16[8,16,1152]{2,1,0:T(8,128)(2,1)} %bitcast.2, bf16[1152,384]{1,0:T(8,128)(2,1)} %weight_in.1, bf16[384,1152]{1,0:T(8,128)(2,1)} %weight_out.1, bf16[8,16,1152]{2,1,0:T(8,128)(2,1)} %bitcast.3), custom_call_target="tpu_custom_call" | custom-call | flops 5436000256 | bytes 8000000 | tf_op jit(solution)/shard_map/pallas_call | solution.py:309
  93.6 2.3 %shard_map.76 = (bf16[16,1152]{1,0:T(8,128)(2,1)}, bf16[16,1152]{1,0:T(8,128)(2,1)}, bf16[1152,384]{1,0:T(8,128)(2,1)}, bf16[384,1152]{1,0:T(8,128)(2,1)}) custom-call(bf16[16,1152]{1,0:T(8,128)(2,1)} %get-tuple-element.8.refs_0_, bf16[16,1152]{1,0:T(8,128)(2,1)} %get-tuple-element.9.refs_1_, bf16[1152,384]{1,0:T(8,128)(2,1)} %get-tuple-element.10.refs_2_, ...), custom_call_target="tpu_custom_call" | custom-call | tf_op jit(solution)/shard_map/pallas_call | solution.py:354
